TPU v7x, 256 devices: a whole 4x4x8 slice. The times are simulated.
256 devices in a mesh: band: 4 (over z_hi, core), grid: 64 (over y, x, z_lo).
Axes of the slice: x: 4, y: 4, z: 8 (z_hi: 2, z_lo: 4; z = z_hi * 4 + z_lo), core: 2. Of those that a mesh axis runs over, the one named last changes fastest.
Arguments:
- orbitals: float32 [8, 128, 128, 128], P('band', 'grid'), may hold values from -6 to 6
- occupation: float32 [8], replicated, may hold values from 0.25 to 2
- kept_modes: int32 [128, 128, 128], P(None, 'grid'), may hold values from 0 to 1, as said below
Outputs:
- exchange_action: float32 [8, 128, 128, 128], P('band', 'grid')
Inputs may be any that keep to these rules, and one draw needn't show every extreme that they name: 0 or 1; kept_modes[a, b, c] is 0 wherever k(a)^2 + k(b)^2 + k(c)^2 > 57^2, with k as in the kernel's step; kept_modes[a, b, c] equals kept_modes[(128 - a) % 128, (128 - b) % 128, (128 - c) % 128].
All inputs are finite; a program needn't handle non-finite values.
Results may differ from a plain program's by a relative error of at most 0.0003.
Values sent between devices are 32-bit elements; how exact they have to be, the bound alone decides.
A program may use at most 64 MiB of HBM per device.

v0:
```python
import functools
import math

import jax
import jax.numpy as jnp
import ml_dtypes
import numpy as np
from jax import lax
from jax.experimental import pallas as pl
from jax.experimental.pallas import tpu as pltpu
from jax.sharding import PartitionSpec as P

MESH = pl.DeviceIdType.MESH
N = 128
PEERS = 64
PITCH = 16
ROWS_O = 15
ROWS_C = 12
LAST_KEPT = 57

E1S, E1R, AS, AR, AFS, FOS, FOR, FCS, FCR, BOS, BOR, BCS, BCR, E2S, E2R, X1S, X1R, DS, DR = range(19)
MR = 19
MS = 22
NSEM = 30


def row_order():
    order = list(range(24)) + [31] + list(range(24, 31)) + list(range(32, 48))
    order += [48, 55] + list(range(49, 55)) + [57, 56]
    return order


def lane_order():
    out = []
    for q in range(4):
        out += [16 * q + i for i in range(16)]
        out += [-16 * q - 16 + i for i in range(16)]
    return out


def split(table):
    high = table.astype(ml_dtypes.bfloat16)
    low = (table - high.astype(np.float64)).astype(ml_dtypes.bfloat16)
    return high, low


def left_table(table):
    high, low = split(table)
    return np.concatenate([high, low, high], axis=1)


def right_table(table):
    high, low = split(table)
    return np.concatenate([high, high, low], axis=0)


def make_tables():
    n = np.arange(N)
    ky = np.array(row_order())
    kz = np.array(lane_order())
    turn = 2.0 * np.pi / N
    angle_y = turn * ((ky[:, None] * n[None, :]) % N)
    forward_y = np.zeros((128, N))
    forward_y[: len(ky)] = np.cos(angle_y)
    forward_y[64 : 64 + len(ky)] = -np.sin(angle_y)
    weight = np.where(ky == 0, 1.0, 2.0)[:, None]
    inverse_y = np.zeros((128, N))
    inverse_y[: len(ky)] = weight * np.cos(angle_y)
    inverse_y[64 : 64 + len(ky)] = -weight * np.sin(angle_y)
    inverse_y = inverse_y.T
    angle_z = turn * ((n[:, None] * kz[None, :]) % N)
    forward_z = np.concatenate([np.cos(angle_z), np.sin(angle_z)], axis=1)
    inverse_z = np.concatenate([np.cos(angle_z.T), np.sin(angle_z.T)], axis=1)
    x = np.concatenate([np.arange(0, N, 2), np.arange(1, N, 2)])
    angle_x = turn * ((n[:, None] * x[None, :]) % N)
    forward_x = np.concatenate([np.cos(angle_x), np.sin(angle_x)], axis=0)
    inverse_x = np.concatenate([np.cos(angle_x.T), np.sin(angle_x.T)], axis=0)
    lanes = np.zeros((N, N))
    lanes[kz % N, np.arange(N)] = 1.0
    return (
        left_table(forward_y),
        right_table(forward_z),
        right_table(inverse_z),
        left_table(inverse_y),
        left_table(forward_x),
        left_table(inverse_x),
        lanes.astype(ml_dtypes.bfloat16),
    )


def dot(a, b):
    return jnp.dot(a, b, preferred_element_type=jnp.float32)


def halves(value):
    high = value.astype(jnp.bfloat16)
    low = (value - high.astype(jnp.float32)).astype(jnp.bfloat16)
    return high, low


def table_times(table, value):
    high, low = halves(value)
    return dot(table, jnp.concatenate([high, high, low], axis=0))


def times_table(value, table):
    high, low = halves(value)
    return dot(jnp.concatenate([high, low, high], axis=1), table)


def lane_ids(rows):
    return lax.broadcasted_iota(jnp.int32, (rows, 128), 1)


def sublane_ids():
    return lax.broadcasted_iota(jnp.int32, (8, 128), 0)


def turn_lanes(value, by):
    return pltpu.roll(value, by % 128, 1)


def quarters(a):
    lane = lane_ids(a[0].shape[0])
    low = lane < 64
    even = (lane // 32) % 2 == 0
    u = [None] * 4
    for k in range(2):
        u[k] = jnp.where(low, a[k], turn_lanes(a[k + 2], 64))
        u[k + 2] = jnp.where(low, turn_lanes(a[k], 64), a[k + 2])
    out = [None] * 4
    for k in (0, 2):
        out[k] = jnp.where(even, u[k], turn_lanes(u[k + 1], 32))
        out[k + 1] = jnp.where(even, turn_lanes(u[k], -32), u[k + 1])
    return out


def to_chunks(q):
    def chunk(g, c):
        return q[g][8 * c : 8 * c + 8]

    sub = sublane_ids()
    mixed_x = jnp.where(sub == 0, chunk(0, 7), chunk(3, 3))
    mixed_y = jnp.where(sub == 1, chunk(0, 7), chunk(1, 6))
    out = [chunk(0, c) for c in range(7)] + [chunk(1, c) for c in range(6)]
    out += [chunk(2, c) for c in range(6)] + [chunk(3, c) for c in range(3)]
    return out + [mixed_x, mixed_y]


def from_chunks(chunks):
    sub = sublane_ids()
    zero = jnp.zeros((8, 128), jnp.float32)
    mixed_x, mixed_y = chunks[22], chunks[23]
    last = jnp.where(sub == 0, mixed_x, jnp.where(sub == 1, mixed_y, zero))
    q0 = chunks[0:7] + [last]
    q1 = chunks[7:13] + [jnp.where(sub == 1, zero, mixed_y), zero]
    q2 = chunks[13:19] + [zero, zero]
    q3 = chunks[19:22] + [jnp.where(sub == 0, zero, mixed_x)] + [zero] * 4
    return [jnp.concatenate(parts, axis=0) for parts in (q0, q1, q2, q3)]


def forward_planes(densities, ty, wz):
    e = table_times(ty, jnp.concatenate(densities, axis=1))
    real, imag = [], []
    for k in range(len(densities)):
        g = times_table(e[:, 128 * k : 128 * k + 128], wz)
        real.append(g[:64, :128] + g[64:, 128:])
        imag.append(g[64:, :128] - g[:64, 128:])
    return real, imag


def inverse_planes(real, imag, wzi, tyi):
    parts = []
    for re, im in zip(real, imag):
        g = times_table(jnp.concatenate([re, im], axis=0), wzi)
        parts.append(
            jnp.concatenate([g[:64, :128] - g[64:, 128:], g[64:, :128] + g[:64, 128:]], axis=0)
        )
    v = table_times(tyi, jnp.concatenate(parts, axis=1))
    return [v[:, 128 * k : 128 * k + 128] for k in range(len(parts))]


def store_chunks(buf, row, chunks):
    for m, value in enumerate(chunks):
        buf[pl.ds((m % 8) * 8 * PITCH + row(m // 8), 8, stride=PITCH), :] = value


def load_chunks(buf, row):
    return [buf[pl.ds((m % 8) * 8 * PITCH + row(m // 8), 8, stride=PITCH), :] for m in range(24)]


def pack_quad(buf, plane, real, imag):
    for ri, part in enumerate((real, imag)):
        store_chunks(buf, lambda j: plane * 6 + j * 2 + ri, to_chunks(quarters(part)))


def unpack_quad(buf, plane):
    return [
        quarters(from_chunks(load_chunks(buf, lambda j: plane * 6 + j * 2 + ri))) for ri in range(2)
    ]


def middle_quad(recv, send, kernel_of, tx, txi):
    blocks = []
    for r in range(6):
        blocks.append(
            jnp.concatenate(
                [recv[pl.ds(plane * 6 + r, 64, stride=PITCH), :] for plane in range(2)], axis=0
            )
        )
    p = table_times(tx, jnp.concatenate(blocks, axis=1))
    c, s = p[:128], p[128:]
    blocks = []
    for j in range(3):
        re, im = slice(256 * j, 256 * j + 128), slice(256 * j + 128, 256 * j + 256)
        blocks.append((c[:, re] + s[:, im]) * kernel_of[j])
        blocks.append((c[:, im] - s[:, re]) * kernel_of[j])
    p = table_times(txi, jnp.concatenate(blocks, axis=1))
    c, s = p[:128], p[128:]
    for j in range(3):
        re, im = slice(256 * j, 256 * j + 128), slice(256 * j + 128, 256 * j + 256)
        new = (c[:, re] - s[:, im], c[:, im] + s[:, re])
        for ri in range(2):
            for plane in range(2):
                send[pl.ds(plane * 6 + j * 2 + ri, 64, stride=PITCH), :] = new[ri][
                    64 * plane : 64 * plane + 64
                ]


def middle_single(recv, send, kernel_of, tx, txi):
    first = lane_ids(128) < 32
    low = lane_ids(64) < 64

    def cross(s):
        return jnp.where(first, turn_lanes(s, -32), -turn_lanes(s, 32))

    blocks = []
    for j in range(3):
        rows = recv[pl.ds(12 + j, 64, stride=PITCH), :]
        blocks.append(jnp.concatenate([rows, turn_lanes(rows, 64)], axis=0))
    p = table_times(tx, jnp.concatenate(blocks, axis=1))
    blocks = []
    for j in range(3):
        at = slice(128 * j, 128 * j + 128)
        blocks.append((p[:128, at] + cross(p[128:, at])) * kernel_of[j])
    p = table_times(txi, jnp.concatenate(blocks, axis=1))
    for j in range(3):
        at = slice(128 * j, 128 * j + 128)
        new = p[:128, at] - cross(p[128:, at])
        send[pl.ds(12 + j, 64, stride=PITCH), :] = jnp.where(
            low, new[:64], turn_lanes(new[64:], 64)
        )


def piece_of(t, j):
    m = j * 8 + t // 8
    sub = t % 8
    q = jnp.where(m < 7, 0, jnp.where(m < 13, 1, jnp.where(m < 19, 2, 3)))
    c = m - jnp.where(m < 7, 0, jnp.where(m < 13, 7, jnp.where(m < 19, 13, 19)))
    is_x = m == 22
    is_y = m == 23
    q = jnp.where(is_y, 1, q)
    c = jnp.where(is_x, 3, jnp.where(is_y, 6, c))
    extra = (is_x & (sub == 0)) | (is_y & (sub == 1))
    q = jnp.where(extra, 0, q)
    c = jnp.where(extra, 7, c)
    pos = c * 8 + sub
    ky = jnp.where((pos >= 25) & (pos <= 31), pos - 1, pos)
    ky = jnp.where((pos >= 50) & (pos <= 55), pos - 1, ky)
    ky = jnp.where(pos == 24, 31, ky)
    ky = jnp.where(pos == 49, 55, ky)
    ky = jnp.where(pos == 56, 57, ky)
    ky = jnp.where(pos == 57, 56, ky)
    return ky, q


def owner_of(ky, q):
    pos = jnp.where((ky >= 24) & (ky <= 30), ky + 1, ky)
    pos = jnp.where((ky >= 49) & (ky <= 54), ky + 1, pos)
    pos = jnp.where(ky == 31, 24, pos)
    pos = jnp.where(ky == 55, 49, pos)
    pos = jnp.where(ky == 57, 56, pos)
    pos = jnp.where(ky == 56, 57, pos)
    c = pos // 8
    sub = pos % 8
    full = jnp.where(q == 0, 7, jnp.where(q == 3, 3, 6))
    base = jnp.where(q == 0, 0, jnp.where(q == 1, 7, jnp.where(q == 2, 13, 19)))
    m = base + c
    m = jnp.where((q == 0) & (c == 7), 22 + sub, m)
    m = jnp.where((q == 1) & (c == 6), 23, m)
    m = jnp.where((q == 3) & (c == 3), 22, m)
    exists = (
        (c < full)
        | ((q == 0) & (c == 7))
        | ((q == 1) & (c == 6) & (sub != 1))
        | ((q == 3) & (c == 3) & (sub != 0))
    ) & (ky <= LAST_KEPT)
    m = jnp.where(exists, m, 0)
    return exists, (m % 8) * 8 + sub, m // 8


def kernel_table(mask, ky, q):
    lane = lane_ids(32)
    rows = []
    for block in range(4):
        part = jnp.where(lane // 32 == block, mask, 0.0)
        part = part + turn_lanes(part, 64)
        rows.append(part + turn_lanes(part, 32))
    kept = jnp.concatenate(rows, axis=0)
    kx = lax.broadcasted_iota(jnp.int32, (128, 128), 0)
    kx = jnp.where(kx < 64, kx, kx - 128)
    i = lane_ids(128) % 32
    kz = jnp.where(i < 16, 16 * q + i, i - 32 - 16 * q)
    squared = kx * kx + ky * ky + kz * kz
    safe = jnp.maximum(squared, 1).astype(jnp.float32)
    return jnp.where(squared > 0, (8.0 * math.pi / N**3) / safe, 0.0) * kept


def body(
    occ, orb, kept, ty, wz, wzi, tyi, tx, txi, lanes, out,
    v, w, x1, pvr, df, act, pv, pf, mask_send, mask_recv,
    f_so, f_ro, b_so, b_ro, f_sc, f_rc, b_sc, b_rc, sem, sem_x, sem_y,
):
    b = lax.axis_index("band")
    g = lax.axis_index("grid")
    half = b // 2
    core = b % 2
    other_core = half * 2 + (1 - core)
    other_half = (1 - half) * 2 + core
    ty, wz, wzi, tyi, tx, txi = (r[...] for r in (ty, wz, wzi, tyi, tx, txi))

    def on_line(stride, k):
        digit = (g // stride) % 4
        return g + ((digit + k) % 4 - digit) * stride

    barrier = pltpu.get_barrier_semaphore()
    for partner in (other_core, other_half):
        pl.semaphore_signal(barrier, inc=1, device_id={"band": partner}, device_id_type=MESH)
    for stride in (1, 4, 16):
        for k in range(1, 4):
            pl.semaphore_signal(
                barrier, inc=1, device_id={"grid": on_line(stride, k)}, device_id_type=MESH
            )
    pl.semaphore_wait(barrier, 11)

    def remote(src, dst, send, recv, band=None, grid=None):
        device = {"band": b if band is None else band, "grid": g if grid is None else grid}
        return pltpu.make_async_remote_copy(
            src_ref=src, dst_ref=dst, send_sem=sem.at[send], recv_sem=sem.at[recv],
            device_id=device, device_id_type=MESH,
        )

    to_core = remote(orb, v, E1S, E1R, band=other_core)
    to_core.start()
    to_half = remote(orb, w, AS, AR, band=other_half)

    @pl.when((half == 0) | (core == 0))
    def _():
        to_half.start()

    for k in range(1, 4):
        pl.semaphore_signal(sem_x, inc=1, device_id={"grid": on_line(4, k)}, device_id_type=MESH)
    pl.semaphore_wait(sem_x, 3)
    for k in range(1, 4):
        pl.semaphore_signal(sem_y, inc=1, device_id={"grid": on_line(16, k)}, device_id_type=MESH)

    for row in range(2):
        plane = dot(kept[:, row, :].astype(jnp.float32).astype(jnp.bfloat16), lanes[...])
        groups = quarters([plane[32 * k : 32 * k + 32] for k in range(4)])
        for q in range(4):
            mask_send[row * 4 + q] = groups[q]
    pl.semaphore_wait(sem_y, 3)

    def mask_copies(act_on_remote, act_on_local):
        def one(i, carry):
            exists, t, j = owner_of(2 * g + i // 4, i % 4)

            @pl.when(exists & (t != g))
            def _():
                act_on_remote(
                    pltpu.make_async_remote_copy(
                        src_ref=mask_send.at[i], dst_ref=mask_recv.at[j],
                        send_sem=sem.at[MS + i], recv_sem=sem.at[MR + j],
                        device_id={"grid": t}, device_id_type=MESH,
                    )
                )

            if act_on_local is not None:

                @pl.when(exists & (t == g))
                def _():
                    act_on_local(
                        pltpu.make_async_copy(mask_send.at[i], mask_recv.at[j], sem.at[MR + j])
                    )

            return carry

        lax.fori_loop(0, 8, one, 0)

    mask_copies(lambda c: c.start(), lambda c: c.start())

    def slot(t, rows):
        return pl.ds(pl.multiple_of(t * PITCH, PITCH), rows)

    def exchange(src, dst, rows, send, recv):
        def one(k, carry):
            t = lax.rem(g + k, PEERS)
            remote(src.at[slot(t, rows)], dst.at[slot(g, rows)], send, recv, grid=t).start()
            return carry

        lax.fori_loop(1, PEERS, one, 0)
        pltpu.make_async_copy(src.at[slot(g, rows)], dst.at[slot(g, rows)], sem.at[recv]).start()

    def arrived(dst, rows, recv):
        whole = dst.at[pl.ds(0, PEERS * rows)]
        pltpu.make_async_copy(whole, whole, sem.at[recv]).wait()

    def sent(src, rows, send):
        whole = src.at[pl.ds(0, (PEERS - 1) * rows)]
        pltpu.make_async_copy(whole, whole, sem.at[send]).wait()

    u = orb
    v0, v1 = core, 1 - core

    to_core.wait_recv()
    for p in range(2):
        d = [u[0, p] * u[0, p], u[0, p] * u[1, p], u[1, p] * u[1, p], u[0, p] * v[v0, p]]
        pack_quad(f_so, p, *forward_planes(d, ty, wz))
    real, imag = forward_planes([u[1, p] * v[v1, p] for p in range(2)], ty, wz)
    store_chunks(f_so, lambda j: 12 + j, to_chunks(quarters([real[0], imag[0], real[1], imag[1]])))
    exchange(f_so, f_ro, ROWS_O, FOS, FOR)

    for j in range(3):
        pltpu.make_async_copy(mask_recv.at[j], mask_recv.at[j], sem.at[MR + j]).wait()
    kernel_of = [kernel_table(mask_recv[j], *piece_of(g, j)) for j in range(3)]

    arrival = pltpu.make_async_copy(w, w, sem.at[AR])
    arrival.wait()
    forward_w = remote(w, w, AFS, AR, band=other_core)

    @pl.when((half == 0) & (core == 0))
    def _():
        forward_w.start()

    near_is_v = (half == 1) & (core == 0)

    def near(i, p):
        return jnp.where(near_is_v, v[i, p], u[i, p])

    for p in range(2):
        d = [near(i, p) * w[j, p] for i in range(2) for j in range(2)]
        pack_quad(f_sc, p, *forward_planes(d, ty, wz))
    exchange(f_sc, f_rc, ROWS_C, FCS, FCR)

    arrived(f_ro, ROWS_O, FOR)
    middle_quad(f_ro, b_so, kernel_of, tx, txi)
    middle_single(f_ro, b_so, kernel_of, tx, txi)
    exchange(b_so, b_ro, ROWS_O, BOS, BOR)
    arrived(f_rc, ROWS_C, FCR)
    middle_quad(f_rc, b_sc, kernel_of, tx, txi)
    exchange(b_sc, b_rc, ROWS_C, BCS, BCR)

    mine = half * 4 + core * 2
    theirs = half * 4 + (1 - core) * 2
    far = (1 - half) * 4 + half * 2 * core
    close = jnp.where(near_is_v, theirs, mine)
    arrived(b_ro, ROWS_O, BOR)
    q = quarters(from_chunks(load_chunks(b_ro, lambda j: 12 + j)))
    lone = inverse_planes([q[0], q[2]], [q[1], q[3]], wzi, tyi)
    for p in range(2):
        pot = inverse_planes(*unpack_quad(b_ro, p), wzi, tyi)
        u0, u1 = u[0, p], u[1, p]
        o0, o1 = occ[mine] * u0, occ[mine + 1] * u1
        act[0, p] = o0 * pot[0] + o1 * pot[1] + occ[theirs + v0] * v[v0, p] * pot[3]
        act[1, p] = o0 * pot[1] + o1 * pot[2] + occ[theirs + v1] * v[v1, p] * lone[p]
        pv[v0, p] = o0 * pot[3]
        pv[v1, p] = o1 * lone[p]

    arrived(b_rc, ROWS_C, BCR)
    for p in range(2):
        pot = inverse_planes(*unpack_quad(b_rc, p), wzi, tyi)
        n0, n1 = near(0, p), near(1, p)
        f0, f1 = occ[far] * w[0, p], occ[far + 1] * w[1, p]
        pf[0, p] = occ[close] * n0 * pot[0] + occ[close + 1] * n1 * pot[2]
        pf[1, p] = occ[close] * n0 * pot[1] + occ[close + 1] * n1 * pot[3]
        for i in range(2):
            term = f0 * pot[2 * i] + f1 * pot[2 * i + 1]
            act[i, p] += jnp.where(near_is_v, 0.0, term)
            pv[i, p] += jnp.where(near_is_v, term, 0.0)

    swap = remote(pv, pvr, E2S, E2R, band=other_core)
    swap.start()
    merge = remote(pf, x1, X1S, X1R, band=other_core)
    home = remote(pf, df, DS, DR, band=other_half)

    @pl.when((half == 0) & (core == 1))
    def _():
        merge.start()

    @pl.when((half == 0) & (core == 0))
    def _():
        merge.wait_recv()
        pf[...] += x1[...]

    @pl.when((half == 1) | (core == 0))
    def _():
        home.start()

    swap.wait_recv()
    for i in range(2):
        for p in range(2):
            act[i, p] += pvr[i, p]

    @pl.when((half == 0) | (core == 0))
    def _():
        home.wait_recv()
        out[...] = -(act[...] + df[...])

    @pl.when((half == 1) & (core == 1))
    def _():
        out[...] = -act[...]

    to_core.wait_send()

    @pl.when((half == 0) | (core == 0))
    def _():
        to_half.wait_send()

    @pl.when((half == 0) & (core == 0))
    def _():
        forward_w.wait_send()

    mask_copies(lambda c: c.wait_send(), None)
    sent(f_so, ROWS_O, FOS)
    sent(f_sc, ROWS_C, FCS)
    sent(b_so, ROWS_O, BOS)
    sent(b_sc, ROWS_C, BCS)
    swap.wait_send()

    @pl.when((half == 0) & (core == 1))
    def _():
        merge.wait_send()

    @pl.when((half == 1) | (core == 0))
    def _():
        home.wait_send()


def on_device(orbitals, occupation, kept_modes):
    block = pltpu.VMEM((2, 2, N, N), jnp.float32)
    message = pltpu.VMEM((PEERS * PITCH, 128), jnp.float32)
    whole = pl.BlockSpec(memory_space=pltpu.VMEM)
    return pl.pallas_call(
        body,
        out_shape=jax.ShapeDtypeStruct(orbitals.shape, jnp.float32),
        in_specs=[pl.BlockSpec(memory_space=pltpu.SMEM)] + [whole] * 9,
        out_specs=whole,
        scratch_shapes=[block] * 8
        + [pltpu.VMEM((8, 32, 128), jnp.float32), pltpu.VMEM((3, 32, 128), jnp.float32)]
        + [message] * 8
        + [
            pltpu.SemaphoreType.DMA((NSEM,)),
            pltpu.SemaphoreType.REGULAR,
            pltpu.SemaphoreType.REGULAR,
        ],
        compiler_params=pltpu.CompilerParams(
            collective_id=1, has_side_effects=True, vmem_limit_bytes=48 << 20
        ),
        name="exchange",
    )(occupation, orbitals, kept_modes, *(jnp.asarray(t) for t in make_tables()))


def solution(mesh):
    return jax.shard_map(
        on_device,
        mesh=mesh,
        in_specs=(P("band", "grid", None, None), P(), P(None, "grid", None)),
        out_specs=P("band", "grid", None, None),
        check_vma=False,
    )
```

profile of v0, /device:TPU:32, one launch (start us, length us, event | category | flops | bytes accessed | tf_op | source)
XLA Modules:
  0.0 86.9 jit_solution(12142476307621706577)
XLA Ops:
  0.0 0.0 copy-start
  0.0 0.9 %copy-done = f32[2,2,128,128]{3,2,1,0:T(8,128)S(1)} copy-done((f32[2,2,128,128]{3,2,1,0:T(8,128)S(1)}, f32[2,2,128,128]{3,2,1,0:T(8,128)}, u32[]{:S(2)}) %copy-start) | copy-done | bytes 262168
  1.0 0.0 copy-start.1
  1.0 0.9 %copy-done.1 = bf16[256,384]{1,0:T(8,128)(2,1)S(1)} copy-done((bf16[256,384]{1,0:T(8,128)(2,1)S(1)}, bf16[256,384]{1,0:T(8,128)(2,1)}, u32[]{:S(2)}) %copy-start.1) | copy-done | bytes 196632
  1.9 0.0 copy-start.2
  1.9 0.9 %copy-done.2 = bf16[256,384]{1,0:T(8,128)(2,1)S(1)} copy-done((bf16[256,384]{1,0:T(8,128)(2,1)S(1)}, bf16[256,384]{1,0:T(8,128)(2,1)}, u32[]{:S(2)}) %copy-start.2) | copy-done | bytes 196632
  2.8 0.0 copy-start.3
  2.8 0.9 %copy-done.3 = bf16[384,256]{1,0:T(8,128)(2,1)S(1)} copy-done((bf16[384,256]{1,0:T(8,128)(2,1)S(1)}, bf16[384,256]{1,0:T(8,128)(2,1)}, u32[]{:S(2)}) %copy-start.3) | copy-done | bytes 196632
  3.7 0.0 copy-start.4
  3.7 0.9 %copy-done.4 = bf16[384,256]{1,0:T(8,128)(2,1)S(1)} copy-done((bf16[384,256]{1,0:T(8,128)(2,1)S(1)}, bf16[384,256]{1,0:T(8,128)(2,1)}, u32[]{:S(2)}) %copy-start.4) | copy-done | bytes 196632
  4.7 0.0 copy-start.5
  4.7 0.9 %copy-done.5 = s32[128,2,128]{2,1,0:T(2,128)S(1)} copy-done((s32[128,2,128]{2,1,0:T(2,128)S(1)}, s32[128,2,128]{2,1,0:T(2,128)}, u32[]{:S(2)}) %copy-start.5) | copy-done | bytes 131096
  5.6 0.0 copy-start.6
  5.6 0.9 %copy-done.6 = bf16[128,384]{1,0:T(8,128)(2,1)S(1)} copy-done((bf16[128,384]{1,0:T(8,128)(2,1)S(1)}, bf16[128,384]{1,0:T(8,128)(2,1)}, u32[]{:S(2)}) %copy-start.6) | copy-done | bytes 98328
  6.5 0.0 copy-start.7
  6.5 0.9 %copy-done.7 = bf16[128,384]{1,0:T(8,128)(2,1)S(1)} copy-done((bf16[128,384]{1,0:T(8,128)(2,1)S(1)}, bf16[128,384]{1,0:T(8,128)(2,1)}, u32[]{:S(2)}) %copy-start.7) | copy-done | bytes 98328
  7.4 0.0 copy-start.8
  7.4 0.8 copy-done.8
  8.1 0.0 copy-start.9
  8.1 0.7 copy-done.9
  8.8 77.4 %exchange.1 = f32[2,2,128,128]{3,2,1,0:T(8,128)S(1)} custom-call(f32[8]{0:T(128)S(1)} %copy-done.9, f32[2,2,128,128]{3,2,1,0:T(8,128)S(1)} %copy-done, s32[128,2,128]{2,1,0:T(2,128)S(1)} %copy-done.5, bf16[128,384]{1,0:T(8,128)(2,1)S(1)} %copy-done.7, bf16[384,256]{1,0:T(8,128)(2,1)S(1)} %copy-done.4, bf16[384,256]{1,0:T(8,128)(2,1)S(1)} %copy-done.3, ...), custom_call_target="tpu_custom_call" | custom-call | tf_op jit(solution)/shard_map/exchange/pallas_call | solution.py:553
  86.2 0.7 copy.12
Async XLA Ops:
  0.0 0.9 %copy-start = (f32[2,2,128,128]{3,2,1,0:T(8,128)S(1)}, f32[2,2,128,128]{3,2,1,0:T(8,128)}, u32[]{:S(2)}) copy-start(f32[2,2,128,128]{3,2,1,0:T(8,128)} %orb.1) | copy-start | bytes 786436
  1.0 0.9 %copy-start.1 = (bf16[256,384]{1,0:T(8,128)(2,1)S(1)}, bf16[256,384]{1,0:T(8,128)(2,1)}, u32[]{:S(2)}) copy-start(bf16[256,384]{1,0:T(8,128)(2,1)} %constant.19.clone.txi) | copy-start | bytes 589828
  1.9 0.9 %copy-start.2 = (bf16[256,384]{1,0:T(8,128)(2,1)S(1)}, bf16[256,384]{1,0:T(8,128)(2,1)}, u32[]{:S(2)}) copy-start(bf16[256,384]{1,0:T(8,128)(2,1)} %constant.18.clone.tx) | copy-start | bytes 589828
  2.8 0.9 %copy-start.3 = (bf16[384,256]{1,0:T(8,128)(2,1)S(1)}, bf16[384,256]{1,0:T(8,128)(2,1)}, u32[]{:S(2)}) copy-start(bf16[384,256]{1,0:T(8,128)(2,1)} %constant.16.clone.wzi) | copy-start | bytes 589828
  3.7 0.9 %copy-start.4 = (bf16[384,256]{1,0:T(8,128)(2,1)S(1)}, bf16[384,256]{1,0:T(8,128)(2,1)}, u32[]{:S(2)}) copy-start(bf16[384,256]{1,0:T(8,128)(2,1)} %constant.15.clone.wz) | copy-start | bytes 589828
  4.7 0.9 %copy-start.5 = (s32[128,2,128]{2,1,0:T(2,128)S(1)}, s32[128,2,128]{2,1,0:T(2,128)}, u32[]{:S(2)}) copy-start(s32[128,2,128]{2,1,0:T(2,128)} %kept.1) | copy-start | bytes 393220
  5.6 0.9 %copy-start.6 = (bf16[128,384]{1,0:T(8,128)(2,1)S(1)}, bf16[128,384]{1,0:T(8,128)(2,1)}, u32[]{:S(2)}) copy-start(bf16[128,384]{1,0:T(8,128)(2,1)} %constant.17.clone.tyi) | copy-start | bytes 294916
  6.5 0.9 %copy-start.7 = (bf16[128,384]{1,0:T(8,128)(2,1)S(1)}, bf16[128,384]{1,0:T(8,128)(2,1)}, u32[]{:S(2)}) copy-start(bf16[128,384]{1,0:T(8,128)(2,1)} %constant.14.clone.ty) | copy-start | bytes 294916
  7.4 0.8 copy-start.8
  8.1 0.7 copy-start.9
where the time goes:
time: 87.3 us; the launch traced here: 86.9 us
  Pallas kernels  77.4 us (89%)
  local copies, waits for them, and re-layouts  9.46 us (11%)
    pallas_call x1, Pallas kernels, on_device(): pl.pallas_call(body, out_shape=jax.ShapeDtypeStruct(orbitals.shape, jnp.f...  77.4 us
    unnamed x21, local copies, waits for them, and re-layouts  9.46 us

commit v1 on v0

--- a/solution.py
+++ b/solution.py
@@ -13,15 +13,18 @@
 MESH = pl.DeviceIdType.MESH
 N = 128
 PEERS = 64
-PITCH = 16
+PITCH_O = 16
 ROWS_O = 15
-ROWS_C = 12
+PITCH_C = 8
+ROWS_C = 6
 LAST_KEPT = 57
 
-E1S, E1R, AS, AR, AFS, FOS, FOR, FCS, FCR, BOS, BOR, BCS, BCR, E2S, E2R, X1S, X1R, DS, DR = range(19)
-MR = 19
-MS = 22
-NSEM = 30
+E1S, E1R, AS, AR, FOS, FOR, FCS, FCR, BOS, BOR, BCS, BCR = range(12)
+E2S, E2R, E3S, E3R, X1S, X1R, DS, DR, MFS, MFR = range(12, 22)
+MR = 22
+MS = 25
+LS = 33
+NSEM = 42
 
 
 def row_order():
@@ -180,32 +183,33 @@
     return [v[:, 128 * k : 128 * k + 128] for k in range(len(parts))]
 
 
-def store_chunks(buf, row, chunks):
+def store_chunks(buf, pitch, row, chunks):
     for m, value in enumerate(chunks):
-        buf[pl.ds((m % 8) * 8 * PITCH + row(m // 8), 8, stride=PITCH), :] = value
-
-
-def load_chunks(buf, row):
-    return [buf[pl.ds((m % 8) * 8 * PITCH + row(m // 8), 8, stride=PITCH), :] for m in range(24)]
-
-
-def pack_quad(buf, plane, real, imag):
+        buf[pl.ds((m % 8) * 8 * pitch + row(m // 8), 8, stride=pitch), :] = value
+
+
+def load_chunks(buf, pitch, row):
+    return [buf[pl.ds((m % 8) * 8 * pitch + row(m // 8), 8, stride=pitch), :] for m in range(24)]
+
+
+def pack_quad(buf, pitch, first, real, imag):
     for ri, part in enumerate((real, imag)):
-        store_chunks(buf, lambda j: plane * 6 + j * 2 + ri, to_chunks(quarters(part)))
-
-
-def unpack_quad(buf, plane):
+        store_chunks(buf, pitch, lambda j: first + j * 2 + ri, to_chunks(quarters(part)))
+
+
+def unpack_quad(buf, pitch, first):
     return [
-        quarters(from_chunks(load_chunks(buf, lambda j: plane * 6 + j * 2 + ri))) for ri in range(2)
+        quarters(from_chunks(load_chunks(buf, pitch, lambda j: first + j * 2 + ri)))
+        for ri in range(2)
     ]
 
 
-def middle_quad(recv, send, kernel_of, tx, txi):
+def middle_quad(recv, send, pitch, second, kernel_of, tx, txi):
     blocks = []
     for r in range(6):
         blocks.append(
             jnp.concatenate(
-                [recv[pl.ds(plane * 6 + r, 64, stride=PITCH), :] for plane in range(2)], axis=0
+                [recv[pl.ds(plane * second + r, 64, stride=pitch), :] for plane in range(2)], axis=0
             )
         )
     p = table_times(tx, jnp.concatenate(blocks, axis=1))
@@ -222,12 +226,12 @@
         new = (c[:, re] - s[:, im], c[:, im] + s[:, re])
         for ri in range(2):
             for plane in range(2):
-                send[pl.ds(plane * 6 + j * 2 + ri, 64, stride=PITCH), :] = new[ri][
+                send[pl.ds(plane * second + j * 2 + ri, 64, stride=pitch), :] = new[ri][
                     64 * plane : 64 * plane + 64
                 ]
 
 
-def middle_single(recv, send, kernel_of, tx, txi):
+def middle_single(recv, send, pitch, kernel_of, tx, txi):
     first = lane_ids(128) < 32
     low = lane_ids(64) < 64
 
@@ -236,7 +240,7 @@
 
     blocks = []
     for j in range(3):
-        rows = recv[pl.ds(12 + j, 64, stride=PITCH), :]
+        rows = recv[pl.ds(12 + j, 64, stride=pitch), :]
         blocks.append(jnp.concatenate([rows, turn_lanes(rows, 64)], axis=0))
     p = table_times(tx, jnp.concatenate(blocks, axis=1))
     blocks = []
@@ -247,7 +251,7 @@
     for j in range(3):
         at = slice(128 * j, 128 * j + 128)
         new = p[:128, at] - cross(p[128:, at])
-        send[pl.ds(12 + j, 64, stride=PITCH), :] = jnp.where(
+        send[pl.ds(12 + j, 64, stride=pitch), :] = jnp.where(
             low, new[:64], turn_lanes(new[64:], 64)
         )
 
@@ -317,8 +321,8 @@
 
 
 def body(
-    occ, orb, kept, ty, wz, wzi, tyi, tx, txi, lanes, out,
-    v, w, x1, pvr, df, act, pv, pf, mask_send, mask_recv,
+    occ, orb_in, kept_in, ty_in, wz_in, wzi_in, tyi_in, tx_in, txi_in, lanes_in, out,
+    chip, kept, ty, wz, wzi, tyi, tx, txi, lanes, far, pvr, df, merged, acc, pf, mask_send, mask_recv,
     f_so, f_ro, b_so, b_ro, f_sc, f_rc, b_sc, b_rc, sem, sem_x, sem_y,
 ):
     b = lax.axis_index("band")
@@ -327,21 +331,38 @@
     core = b % 2
     other_core = half * 2 + (1 - core)
     other_half = (1 - half) * 2 + core
-    ty, wz, wzi, tyi, tx, txi = (r[...] for r in (ty, wz, wzi, tyi, tx, txi))
+
+    u, v = chip.at[0], chip.at[1]
+    act, pv = acc.at[0], acc.at[1]
+    loads = [
+        pltpu.make_async_copy(source, target, sem.at[LS + i])
+        for i, (source, target) in enumerate(
+            [
+                (orb_in, u), (ty_in, ty), (wz_in, wz), (kept_in, kept), (lanes_in, lanes),
+                (tx_in, tx), (txi_in, txi), (wzi_in, wzi), (tyi_in, tyi),
+            ]
+        )
+    ]
+    for load in loads:
+        load.start()
 
     def on_line(stride, k):
         digit = (g // stride) % 4
         return g + ((digit + k) % 4 - digit) * stride
 
     barrier = pltpu.get_barrier_semaphore()
-    for partner in (other_core, other_half):
-        pl.semaphore_signal(barrier, inc=1, device_id={"band": partner}, device_id_type=MESH)
+
+    def greet(semaphore, band, grid):
+        pl.semaphore_signal(
+            semaphore, inc=1, device_id={"band": band, "grid": grid}, device_id_type=MESH
+        )
+
+    for k in range(4):
+        greet(barrier, other_half, on_line(1, k))
     for stride in (1, 4, 16):
         for k in range(1, 4):
-            pl.semaphore_signal(
-                barrier, inc=1, device_id={"grid": on_line(stride, k)}, device_id_type=MESH
-            )
-    pl.semaphore_wait(barrier, 11)
+            greet(barrier, b, on_line(stride, k))
+    greet(barrier, other_core, g)
 
     def remote(src, dst, send, recv, band=None, grid=None):
         device = {"band": b if band is None else band, "grid": g if grid is None else grid}
@@ -350,25 +371,43 @@
             device_id=device, device_id_type=MESH,
         )
 
-    to_core = remote(orb, v, E1S, E1R, band=other_core)
+    for load in loads[:3]:
+        load.wait()
+    ty, wz = ty[...], wz[...]
+    own = [
+        forward_planes([u[0, p] * u[0, p], u[0, p] * u[1, p], u[1, p] * u[1, p]], ty, wz)
+        for p in range(2)
+    ]
+
+    pl.semaphore_wait(barrier, 14)
+    to_core = remote(u, v, E1S, E1R, band=other_core)
     to_core.start()
-    to_half = remote(orb, w, AS, AR, band=other_half)
-
-    @pl.when((half == 0) | (core == 0))
-    def _():
-        to_half.start()
-
+    to_half = remote(u.at[:, 1 - half], far.at[0], AS, AR, band=other_half)
+    to_half.start()
     for k in range(1, 4):
-        pl.semaphore_signal(sem_x, inc=1, device_id={"grid": on_line(4, k)}, device_id_type=MESH)
-    pl.semaphore_wait(sem_x, 3)
-    for k in range(1, 4):
-        pl.semaphore_signal(sem_y, inc=1, device_id={"grid": on_line(16, k)}, device_id_type=MESH)
-
+        greet(sem_x, b, on_line(4, k))
+
+    for load in loads[3:]:
+        load.wait()
+    tx, txi, wzi, tyi = tx[...], txi[...], wzi[...], tyi[...]
     for row in range(2):
         plane = dot(kept[:, row, :].astype(jnp.float32).astype(jnp.bfloat16), lanes[...])
         groups = quarters([plane[32 * k : 32 * k + 32] for k in range(4)])
         for q in range(4):
             mask_send[row * 4 + q] = groups[q]
+    pl.semaphore_wait(sem_x, 3)
+    for k in range(1, 4):
+        greet(sem_y, b, on_line(16, k))
+
+    v0, v1 = core, 1 - core
+    to_core.wait_recv()
+    real, imag = forward_planes(
+        [u[0, p] * v[v0, p] for p in range(2)] + [u[1, p] * v[v1, p] for p in range(2)], ty, wz
+    )
+    for p in range(2):
+        pack_quad(f_so, PITCH_O, p * 6, own[p][0] + [real[p]], own[p][1] + [imag[p]])
+    lone = quarters([real[2], imag[2], real[3], imag[3]])
+    store_chunks(f_so, PITCH_O, lambda j: 12 + j, to_chunks(lone))
     pl.semaphore_wait(sem_y, 3)
 
     def mask_copies(act_on_remote, act_on_local):
@@ -381,7 +420,7 @@
                     pltpu.make_async_remote_copy(
                         src_ref=mask_send.at[i], dst_ref=mask_recv.at[j],
                         send_sem=sem.at[MS + i], recv_sem=sem.at[MR + j],
-                        device_id={"grid": t}, device_id_type=MESH,
+                        device_id={"band": b, "grid": t}, device_id_type=MESH,
                     )
                 )
 
@@ -397,78 +436,91 @@
 
         lax.fori_loop(0, 8, one, 0)
 
-    mask_copies(lambda c: c.start(), lambda c: c.start())
-
-    def slot(t, rows):
-        return pl.ds(pl.multiple_of(t * PITCH, PITCH), rows)
-
-    def exchange(src, dst, rows, send, recv):
+    mask_to_core = remote(mask_recv, mask_recv, MFS, MFR, band=other_core)
+
+    @pl.when(core == 0)
+    def _():
+        mask_copies(lambda c: c.start(), lambda c: c.start())
+
+    def slot(index, pitch, rows):
+        return pl.ds(pl.multiple_of(index * pitch, pitch), rows)
+
+    def exchange_own(src, dst, send, recv):
         def one(k, carry):
             t = lax.rem(g + k, PEERS)
-            remote(src.at[slot(t, rows)], dst.at[slot(g, rows)], send, recv, grid=t).start()
+            remote(
+                src.at[slot(t, PITCH_O, ROWS_O)], dst.at[slot(g, PITCH_O, ROWS_O)], send, recv, grid=t
+            ).start()
             return carry
 
         lax.fori_loop(1, PEERS, one, 0)
-        pltpu.make_async_copy(src.at[slot(g, rows)], dst.at[slot(g, rows)], sem.at[recv]).start()
+        me = slot(g, PITCH_O, ROWS_O)
+        pltpu.make_async_copy(src.at[me], dst.at[me], sem.at[recv]).start()
+
+    def exchange_cross(src, dst, send, recv):
+        index = half * PEERS + g
+        me = slot(index, PITCH_C, ROWS_C)
+
+        def one(k, carry):
+            t = lax.rem(index + k, 2 * PEERS)
+            remote(
+                src.at[slot(t, PITCH_C, ROWS_C)], dst.at[me], send, recv,
+                band=(t // PEERS) * 2 + core, grid=t % PEERS,
+            ).start()
+            return carry
+
+        lax.fori_loop(1, 2 * PEERS, one, 0)
+        pltpu.make_async_copy(src.at[me], dst.at[me], sem.at[recv]).start()
 
     def arrived(dst, rows, recv):
-        whole = dst.at[pl.ds(0, PEERS * rows)]
+        whole = dst.at[pl.ds(0, rows)]
         pltpu.make_async_copy(whole, whole, sem.at[recv]).wait()
 
-    def sent(src, rows, send):
-        whole = src.at[pl.ds(0, (PEERS - 1) * rows)]
-        pltpu.make_async_copy(whole, whole, sem.at[send]).wait()
-
-    u = orb
-    v0, v1 = core, 1 - core
-
-    to_core.wait_recv()
-    for p in range(2):
-        d = [u[0, p] * u[0, p], u[0, p] * u[1, p], u[1, p] * u[1, p], u[0, p] * v[v0, p]]
-        pack_quad(f_so, p, *forward_planes(d, ty, wz))
-    real, imag = forward_planes([u[1, p] * v[v1, p] for p in range(2)], ty, wz)
-    store_chunks(f_so, lambda j: 12 + j, to_chunks(quarters([real[0], imag[0], real[1], imag[1]])))
-    exchange(f_so, f_ro, ROWS_O, FOS, FOR)
-
-    for j in range(3):
-        pltpu.make_async_copy(mask_recv.at[j], mask_recv.at[j], sem.at[MR + j]).wait()
+    exchange_own(f_so, f_ro, FOS, FOR)
+
+    @pl.when(core == 0)
+    def _():
+        for j in range(3):
+            pltpu.make_async_copy(mask_recv.at[j], mask_recv.at[j], sem.at[MR + j]).wait()
+        mask_to_core.start()
+
+    @pl.when(core == 1)
+    def _():
+        mask_to_core.wait_recv()
+
     kernel_of = [kernel_table(mask_recv[j], *piece_of(g, j)) for j in range(3)]
 
-    arrival = pltpu.make_async_copy(w, w, sem.at[AR])
-    arrival.wait()
-    forward_w = remote(w, w, AFS, AR, band=other_core)
-
-    @pl.when((half == 0) & (core == 0))
-    def _():
-        forward_w.start()
-
-    near_is_v = (half == 1) & (core == 0)
-
-    def near(i, p):
-        return jnp.where(near_is_v, v[i, p], u[i, p])
-
-    for p in range(2):
-        d = [near(i, p) * w[j, p] for i in range(2) for j in range(2)]
-        pack_quad(f_sc, p, *forward_planes(d, ty, wz))
-    exchange(f_sc, f_rc, ROWS_C, FCS, FCR)
-
-    arrived(f_ro, ROWS_O, FOR)
-    middle_quad(f_ro, b_so, kernel_of, tx, txi)
-    middle_single(f_ro, b_so, kernel_of, tx, txi)
-    exchange(b_so, b_ro, ROWS_O, BOS, BOR)
-    arrived(f_rc, ROWS_C, FCR)
-    middle_quad(f_rc, b_sc, kernel_of, tx, txi)
-    exchange(b_sc, b_rc, ROWS_C, BCS, BCR)
+    first_quad = half * core
+    quads = ((first_quad, 0, core), (1 - first_quad, 1, 1 - core))
+
+    def pack_cross(quad, f, n):
+        near = [chip[n, i, half] for i in (0, half, 1 - half, 1)]
+        d = [a * far[f, i] for a, i in zip(near, (0, 1 - half, half, 1))]
+        pack_quad(f_sc, PITCH_C, quad * (PEERS * PITCH_C), *forward_planes(d, ty, wz))
+
+    to_half.wait_recv()
+    far_to_core = remote(far.at[0], far.at[1], E3S, E3R, band=other_core)
+    far_to_core.start()
+    pack_cross(*quads[0])
+    far_to_core.wait_recv()
+    pack_cross(*quads[1])
+    exchange_cross(f_sc, f_rc, FCS, FCR)
+
+    arrived(f_ro, PEERS * ROWS_O, FOR)
+    middle_quad(f_ro, b_so, PITCH_O, 6, kernel_of, tx, txi)
+    middle_single(f_ro, b_so, PITCH_O, kernel_of, tx, txi)
+    exchange_own(b_so, b_ro, BOS, BOR)
+    arrived(f_rc, 2 * PEERS * ROWS_C, FCR)
+    middle_quad(f_rc, b_sc, PITCH_C, PEERS * PITCH_C, kernel_of, tx, txi)
+    exchange_cross(b_sc, b_rc, BCS, BCR)
 
     mine = half * 4 + core * 2
     theirs = half * 4 + (1 - core) * 2
-    far = (1 - half) * 4 + half * 2 * core
-    close = jnp.where(near_is_v, theirs, mine)
-    arrived(b_ro, ROWS_O, BOR)
-    q = quarters(from_chunks(load_chunks(b_ro, lambda j: 12 + j)))
+    arrived(b_ro, PEERS * ROWS_O, BOR)
+    q = quarters(from_chunks(load_chunks(b_ro, PITCH_O, lambda j: 12 + j)))
     lone = inverse_planes([q[0], q[2]], [q[1], q[3]], wzi, tyi)
     for p in range(2):
-        pot = inverse_planes(*unpack_quad(b_ro, p), wzi, tyi)
+        pot = inverse_planes(*unpack_quad(b_ro, PITCH_O, p * 6), wzi, tyi)
         u0, u1 = u[0, p], u[1, p]
         o0, o1 = occ[mine] * u0, occ[mine + 1] * u1
         act[0, p] = o0 * pot[0] + o1 * pot[1] + occ[theirs + v0] * v[v0, p] * pot[3]
@@ -476,86 +528,76 @@
         pv[v0, p] = o0 * pot[3]
         pv[v1, p] = o1 * lone[p]
 
-    arrived(b_rc, ROWS_C, BCR)
-    for p in range(2):
-        pot = inverse_planes(*unpack_quad(b_rc, p), wzi, tyi)
-        n0, n1 = near(0, p), near(1, p)
-        f0, f1 = occ[far] * w[0, p], occ[far + 1] * w[1, p]
-        pf[0, p] = occ[close] * n0 * pot[0] + occ[close + 1] * n1 * pot[2]
-        pf[1, p] = occ[close] * n0 * pot[1] + occ[close + 1] * n1 * pot[3]
-        for i in range(2):
-            term = f0 * pot[2 * i] + f1 * pot[2 * i + 1]
-            act[i, p] += jnp.where(near_is_v, 0.0, term)
-            pv[i, p] += jnp.where(near_is_v, term, 0.0)
-
+    arrived(b_rc, 2 * PEERS * ROWS_C, BCR)
+
+    def cross_terms(quad, f, n):
+        first = quad * (PEERS * PITCH_C)
+        p00, p01, p10, p11 = inverse_planes(*unpack_quad(b_rc, PITCH_C, first), wzi, tyi)
+        p01, p10 = jnp.where(half == 0, p01, p10), jnp.where(half == 0, p10, p01)
+        here = half * 4 + jnp.where(n == 0, core, 1 - core) * 2
+        there = (1 - half) * 4 + (core if f == 0 else 1 - core) * 2
+        n0, n1 = occ[here] * chip[n, 0, half], occ[here + 1] * chip[n, 1, half]
+        f0, f1 = occ[there] * far[f, 0], occ[there + 1] * far[f, 1]
+        pf[f, 0] = n0 * p00 + n1 * p10
+        pf[f, 1] = n0 * p01 + n1 * p11
+        acc[n, 0, half] += f0 * p00 + f1 * p01
+        acc[n, 1, half] += f0 * p10 + f1 * p11
+
+    cross_terms(*quads[1])
+    merge = remote(pf.at[1], merged, X1S, X1R, band=other_core)
+    merge.start()
+    cross_terms(*quads[0])
+    merge.wait_recv()
+    pf[0] += merged[...]
+    home = remote(pf.at[0], df, DS, DR, band=other_half)
+    home.start()
     swap = remote(pv, pvr, E2S, E2R, band=other_core)
     swap.start()
-    merge = remote(pf, x1, X1S, X1R, band=other_core)
-    home = remote(pf, df, DS, DR, band=other_half)
-
-    @pl.when((half == 0) & (core == 1))
-    def _():
-        merge.start()
-
-    @pl.when((half == 0) & (core == 0))
-    def _():
-        merge.wait_recv()
-        pf[...] += x1[...]
-
-    @pl.when((half == 1) | (core == 0))
-    def _():
-        home.start()
-
     swap.wait_recv()
     for i in range(2):
-        for p in range(2):
-            act[i, p] += pvr[i, p]
-
-    @pl.when((half == 0) | (core == 0))
+        out[i, half] = -(act[i, half] + pvr[i, half])
+        acc[0, i, 1 - half] += pvr[i, 1 - half]
+    home.wait_recv()
+    for i in range(2):
+        out[i, 1 - half] = -(act[i, 1 - half] + df[i])
+
+    to_core.wait_send()
+    to_half.wait_send()
+
+    @pl.when(core == 0)
     def _():
-        home.wait_recv()
-        out[...] = -(act[...] + df[...])
-
-    @pl.when((half == 1) & (core == 1))
-    def _():
-        out[...] = -act[...]
-
-    to_core.wait_send()
-
-    @pl.when((half == 0) | (core == 0))
-    def _():
-        to_half.wait_send()
-
-    @pl.when((half == 0) & (core == 0))
-    def _():
-        forward_w.wait_send()
-
-    mask_copies(lambda c: c.wait_send(), None)
-    sent(f_so, ROWS_O, FOS)
-    sent(f_sc, ROWS_C, FCS)
-    sent(b_so, ROWS_O, BOS)
-    sent(b_sc, ROWS_C, BCS)
+        mask_to_core.wait_send()
+        mask_copies(lambda c: c.wait_send(), None)
+
+    for src, rows, send in (
+        (f_so, (PEERS - 1) * ROWS_O, FOS),
+        (f_sc, (2 * PEERS - 1) * ROWS_C, FCS),
+        (b_so, (PEERS - 1) * ROWS_O, BOS),
+        (b_sc, (2 * PEERS - 1) * ROWS_C, BCS),
+    ):
+        arrived(src, rows, send)
+    far_to_core.wait_send()
+    merge.wait_send()
     swap.wait_send()
-
-    @pl.when((half == 0) & (core == 1))
-    def _():
-        merge.wait_send()
-
-    @pl.when((half == 1) | (core == 0))
-    def _():
-        home.wait_send()
+    home.wait_send()
 
 
 def on_device(orbitals, occupation, kept_modes):
     block = pltpu.VMEM((2, 2, N, N), jnp.float32)
-    message = pltpu.VMEM((PEERS * PITCH, 128), jnp.float32)
-    whole = pl.BlockSpec(memory_space=pltpu.VMEM)
+    twice = pltpu.VMEM((2, 2, 2, N, N), jnp.float32)
+    plane = pltpu.VMEM((2, N, N), jnp.float32)
+    planes = pltpu.VMEM((2, 2, N, N), jnp.float32)
+    message = pltpu.VMEM((PEERS * PITCH_O, 128), jnp.float32)
+    tables = make_tables()
+    loaded = [twice, pltpu.VMEM(kept_modes.shape, jnp.int32)]
+    loaded += [pltpu.VMEM(t.shape, jnp.bfloat16) for t in tables]
     return pl.pallas_call(
         body,
         out_shape=jax.ShapeDtypeStruct(orbitals.shape, jnp.float32),
-        in_specs=[pl.BlockSpec(memory_space=pltpu.SMEM)] + [whole] * 9,
-        out_specs=whole,
-        scratch_shapes=[block] * 8
+        in_specs=[pl.BlockSpec(memory_space=pltpu.SMEM)] + [pl.BlockSpec(memory_space=pl.ANY)] * 9,
+        out_specs=pl.BlockSpec(memory_space=pltpu.VMEM),
+        scratch_shapes=loaded
+        + [planes, block, plane, plane, twice, planes]
         + [pltpu.VMEM((8, 32, 128), jnp.float32), pltpu.VMEM((3, 32, 128), jnp.float32)]
         + [message] * 8
         + [
@@ -564,10 +606,10 @@
             pltpu.SemaphoreType.REGULAR,
         ],
         compiler_params=pltpu.CompilerParams(
-            collective_id=1, has_side_effects=True, vmem_limit_bytes=48 << 20
+            collective_id=1, has_side_effects=True, vmem_limit_bytes=60 << 20
         ),
         name="exchange",
-    )(occupation, orbitals, kept_modes, *(jnp.asarray(t) for t in make_tables()))
+    )(occupation, orbitals, kept_modes, *(jnp.asarray(t) for t in tables))
 
 
 def solution(mesh):

time: 87.3 us -> 74 us (0.85)
  the two profiles are of different devices: /device:TPU:32 before, /device:TPU:1 now
where the time goes in v1:
time: 74 us; the launch traced here: 73.8 us
  Pallas kernels  72.2 us (98%)
  local copies, waits for them, and re-layouts  1.67 us (2%)
    pallas_call x1, Pallas kernels, on_device(): pl.pallas_call(body, out_shape=jax.ShapeDtypeStruct(orbitals.shape, jnp.f...  72.2 us
    unnamed x1, local copies, waits for them, and re-layouts  1.67 us

profile of v1, /device:TPU:1, one launch (start us, length us, event | category | flops | bytes accessed | tf_op | source)
XLA Modules:
  0.0 73.8 jit_solution(7341342651636885863)
XLA Ops:
  0.0 72.2 %exchange.1 = f32[2,2,128,128]{3,2,1,0:T(8,128)} custom-call(f32[8]{0:T(128)} %occ.1, f32[2,2,128,128]{3,2,1,0:T(8,128)} %orb_in.1, s32[128,2,128]{2,1,0:T(2,128)} %kept_in.1, bf16[128,384]{1,0:T(8,128)(2,1)} %constant.14.clone.ty_in, bf16[384,256]{1,0:T(8,128)(2,1)} %constant.15.clone.wz_in, bf16[384,256]{1,0:T(8,128)(2,1)} %constant.16.clone.wzi_in, ...), custom_call_target="tpu_custom_call" | custom-call | tf_op jit(solution)/shard_map/exchange/pallas_call | solution.py:594
  72.2 1.7 %copy.12 = f32[2,2,128,128]{3,2,1,0:T(8,128)} copy(f32[2,2,128,128]{3,2,1,0:T(8,128)} %exchange.1) | data formatting | bytes 524288

commit v2 on v1

--- a/solution.py
+++ b/solution.py
@@ -13,18 +13,18 @@
 MESH = pl.DeviceIdType.MESH
 N = 128
 PEERS = 64
-PITCH_O = 16
-ROWS_O = 15
-PITCH_C = 8
-ROWS_C = 6
+ROWS_1, PITCH_1 = 9, 16
+ROWS_2, PITCH_2 = 6, 8
+ROWS_C, PITCH_C = 6, 8
 LAST_KEPT = 57
-
-E1S, E1R, AS, AR, FOS, FOR, FCS, FCR, BOS, BOR, BCS, BCR = range(12)
-E2S, E2R, E3S, E3R, X1S, X1R, DS, DR, MFS, MFR = range(12, 22)
-MR = 22
-MS = 25
-LS = 33
-NSEM = 42
+CUTS = 8
+
+E1S, E1R, AS, AR, F1S, F1R, F2S, F2R, FCS, FCR, B1S, B1R, B2S, B2R, BCS, BCR = range(16)
+E2S, E2R, E3S, E3R, X1S, X1R, DS, DR, MFS, MFR = range(16, 26)
+MR = 26
+MS = 29
+LS = 37
+NSEM = 46
 
 
 def row_order():
@@ -197,51 +197,76 @@
         store_chunks(buf, pitch, lambda j: first + j * 2 + ri, to_chunks(quarters(part)))
 
 
-def unpack_quad(buf, pitch, first):
-    return [
-        quarters(from_chunks(load_chunks(buf, pitch, lambda j: first + j * 2 + ri)))
-        for ri in range(2)
-    ]
-
-
-def middle_quad(recv, send, pitch, second, kernel_of, tx, txi):
-    blocks = []
-    for r in range(6):
-        blocks.append(
-            jnp.concatenate(
-                [recv[pl.ds(plane * second + r, 64, stride=pitch), :] for plane in range(2)], axis=0
-            )
-        )
-    p = table_times(tx, jnp.concatenate(blocks, axis=1))
+def unpack(buf, pitch, row):
+    return quarters(from_chunks(load_chunks(buf, pitch, row)))
+
+
+def spectrum(buf, pitch, second, row):
+    return jnp.concatenate(
+        [buf[pl.ds(plane * second + row, 64, stride=pitch), :] for plane in range(2)], axis=0
+    )
+
+
+def convolve(real, imag, kernel_of, tx, txi):
+    p = table_times(tx, jnp.concatenate(real + imag, axis=1))
     c, s = p[:128], p[128:]
     blocks = []
     for j in range(3):
-        re, im = slice(256 * j, 256 * j + 128), slice(256 * j + 128, 256 * j + 256)
+        re, im = slice(128 * j, 128 * j + 128), slice(384 + 128 * j, 512 + 128 * j)
         blocks.append((c[:, re] + s[:, im]) * kernel_of[j])
+    for j in range(3):
+        re, im = slice(128 * j, 128 * j + 128), slice(384 + 128 * j, 512 + 128 * j)
         blocks.append((c[:, im] - s[:, re]) * kernel_of[j])
     p = table_times(txi, jnp.concatenate(blocks, axis=1))
     c, s = p[:128], p[128:]
+    real, imag = [], []
     for j in range(3):
-        re, im = slice(256 * j, 256 * j + 128), slice(256 * j + 128, 256 * j + 256)
-        new = (c[:, re] - s[:, im], c[:, im] + s[:, re])
-        for ri in range(2):
+        re, im = slice(128 * j, 128 * j + 128), slice(384 + 128 * j, 512 + 128 * j)
+        real.append(c[:, re] - s[:, im])
+        imag.append(c[:, im] + s[:, re])
+    return real, imag
+
+
+def middle_cross(recv, send, kernel_of, tx, txi):
+    second = PEERS * PITCH_C
+    parts = [[spectrum(recv, PITCH_C, second, j * 2 + ri) for j in range(3)] for ri in range(2)]
+    for ri, new in enumerate(convolve(*parts, kernel_of, tx, txi)):
+        for j in range(3):
             for plane in range(2):
-                send[pl.ds(plane * second + j * 2 + ri, 64, stride=pitch), :] = new[ri][
+                send[pl.ds(plane * second + j * 2 + ri, 64, stride=PITCH_C), :] = new[j][
                     64 * plane : 64 * plane + 64
                 ]
 
 
-def middle_single(recv, send, pitch, kernel_of, tx, txi):
-    first = lane_ids(128) < 32
-    low = lane_ids(64) < 64
+def middle_first(recv, send, kernel_of, tx, txi):
+    lane = lane_ids(64)
+    real, imag = [], []
+    for j in range(3):
+        r0, r1, r2 = (recv[pl.ds(j * 3 + i, 64, stride=PITCH_1), :] for i in range(3))
+        real.append(jnp.concatenate([r0, r1], axis=0))
+        i0 = jnp.where(lane < 32, turn_lanes(r0, 32), turn_lanes(r2, 32))
+        i1 = jnp.where(lane < 32, turn_lanes(r1, 32), turn_lanes(r2, -32))
+        imag.append(jnp.concatenate([i0, i1], axis=0))
+    real, imag = convolve(real, imag, kernel_of, tx, txi)
+    for j in range(3):
+        i0, i1 = imag[j][:64], imag[j][64:]
+        rows = (
+            jnp.where(lane < 96, real[j][:64], turn_lanes(i0, 96)),
+            jnp.where(lane < 96, real[j][64:], turn_lanes(i1, 96)),
+            jnp.where(lane < 64, turn_lanes(i0, -32), turn_lanes(i1, 32)),
+        )
+        for i in range(3):
+            send[pl.ds(j * 3 + i, 64, stride=PITCH_1), :] = rows[i]
+
+
+def middle_second(recv, send, kernel_of, tx, txi):
+    low = lane_ids(128) < 64
 
     def cross(s):
-        return jnp.where(first, turn_lanes(s, -32), -turn_lanes(s, 32))
-
-    blocks = []
-    for j in range(3):
-        rows = recv[pl.ds(12 + j, 64, stride=pitch), :]
-        blocks.append(jnp.concatenate([rows, turn_lanes(rows, 64)], axis=0))
+        turned = turn_lanes(s, 64)
+        return jnp.where(low, turned, -turned)
+
+    blocks = [spectrum(recv, PITCH_2, 1, j * 2) for j in range(3)]
     p = table_times(tx, jnp.concatenate(blocks, axis=1))
     blocks = []
     for j in range(3):
@@ -251,9 +276,8 @@
     for j in range(3):
         at = slice(128 * j, 128 * j + 128)
         new = p[:128, at] - cross(p[128:, at])
-        send[pl.ds(12 + j, 64, stride=pitch), :] = jnp.where(
-            low, new[:64], turn_lanes(new[64:], 64)
-        )
+        for plane in range(2):
+            send[pl.ds(j * 2 + plane, 64, stride=PITCH_2), :] = new[64 * plane : 64 * plane + 64]
 
 
 def piece_of(t, j):
@@ -323,7 +347,7 @@
 def body(
     occ, orb_in, kept_in, ty_in, wz_in, wzi_in, tyi_in, tx_in, txi_in, lanes_in, out,
     chip, kept, ty, wz, wzi, tyi, tx, txi, lanes, far, pvr, df, merged, acc, pf, mask_send, mask_recv,
-    f_so, f_ro, b_so, b_ro, f_sc, f_rc, b_sc, b_rc, sem, sem_x, sem_y,
+    f_s1, f_r1, b_s1, b_r1, f_s2, f_r2, b_s2, b_r2, f_sc, f_rc, b_sc, b_rc, sem, sem_xy,
 ):
     b = lax.axis_index("band")
     g = lax.axis_index("grid")
@@ -346,9 +370,11 @@
     for load in loads:
         load.start()
 
-    def on_line(stride, k):
-        digit = (g // stride) % 4
-        return g + ((digit + k) % 4 - digit) * stride
+    def on_line(k):
+        return g - g % 4 + (g + k) % 4
+
+    def in_plane(k):
+        return ((g // 4 + k) % 16) * 4 + g % 4
 
     barrier = pltpu.get_barrier_semaphore()
 
@@ -358,10 +384,11 @@
         )
 
     for k in range(4):
-        greet(barrier, other_half, on_line(1, k))
-    for stride in (1, 4, 16):
-        for k in range(1, 4):
-            greet(barrier, b, on_line(stride, k))
+        greet(barrier, other_half, on_line(k))
+    for k in range(1, 4):
+        greet(barrier, b, on_line(k))
+    for k in range(1, 16):
+        greet(barrier, b, in_plane(k))
     greet(barrier, other_core, g)
 
     def remote(src, dst, send, recv, band=None, grid=None):
@@ -371,7 +398,35 @@
             device_id=device, device_id_type=MESH,
         )
 
-    for load in loads[:3]:
+    class Cut:
+        def __init__(self, src, dst, send, recv, band):
+            self.parts = [
+                remote(src.at[i, pl.ds(r, N // CUTS)], dst.at[i, pl.ds(r, N // CUTS)], send, recv, band=band)
+                for r in range(0, N, N // CUTS)
+                for i in range(2)
+            ]
+            self.whole = remote(src, dst, send, recv, band=band)
+
+        def start(self):
+            for part in self.parts:
+                part.start()
+
+        def wait_recv(self):
+            self.whole.wait_recv()
+
+        def wait_send(self):
+            self.whole.wait_send()
+
+    pl.semaphore_wait(barrier, 23)
+    for k in range(1, 16):
+        greet(sem_xy, b, in_plane(k))
+    loads[0].wait()
+    to_half = Cut(u.at[:, 1 - half], far.at[0], AS, AR, other_half)
+    to_half.start()
+    to_core = remote(u, v, E1S, E1R, band=other_core)
+    to_core.start()
+
+    for load in loads[1:3]:
         load.wait()
     ty, wz = ty[...], wz[...]
     own = [
@@ -379,13 +434,12 @@
         for p in range(2)
     ]
 
-    pl.semaphore_wait(barrier, 14)
-    to_core = remote(u, v, E1S, E1R, band=other_core)
-    to_core.start()
-    to_half = remote(u.at[:, 1 - half], far.at[0], AS, AR, band=other_half)
-    to_half.start()
-    for k in range(1, 4):
-        greet(sem_x, b, on_line(4, k))
+    for p in range(2):
+        real, imag = own[p]
+        chunks = to_chunks(quarters(real + imag[:1]))
+        store_chunks(f_s1, PITCH_1, lambda j: j * 3 + p, chunks)
+    chunks = to_chunks(quarters(own[0][1][1:] + own[1][1][1:]))
+    store_chunks(f_s1, PITCH_1, lambda j: j * 3 + 2, chunks)
 
     for load in loads[3:]:
         load.wait()
@@ -395,20 +449,6 @@
         groups = quarters([plane[32 * k : 32 * k + 32] for k in range(4)])
         for q in range(4):
             mask_send[row * 4 + q] = groups[q]
-    pl.semaphore_wait(sem_x, 3)
-    for k in range(1, 4):
-        greet(sem_y, b, on_line(16, k))
-
-    v0, v1 = core, 1 - core
-    to_core.wait_recv()
-    real, imag = forward_planes(
-        [u[0, p] * v[v0, p] for p in range(2)] + [u[1, p] * v[v1, p] for p in range(2)], ty, wz
-    )
-    for p in range(2):
-        pack_quad(f_so, PITCH_O, p * 6, own[p][0] + [real[p]], own[p][1] + [imag[p]])
-    lone = quarters([real[2], imag[2], real[3], imag[3]])
-    store_chunks(f_so, PITCH_O, lambda j: 12 + j, to_chunks(lone))
-    pl.semaphore_wait(sem_y, 3)
 
     def mask_copies(act_on_remote, act_on_local):
         def one(i, carry):
@@ -438,46 +478,84 @@
 
     mask_to_core = remote(mask_recv, mask_recv, MFS, MFR, band=other_core)
 
+    def peer(k):
+        z = (g + jnp.where(k < 16, 2, jnp.where(k < 32, 1, jnp.where(k < 48, 3, 0)))) % 4
+        return ((g // 4 + k + jnp.where(k < 48, 0, 1)) % 16) * 4 + z
+
+    def slot(index, pitch, rows):
+        return pl.ds(pl.multiple_of(index * pitch, pitch), rows)
+
+    def exchange(src, dst, pitch, rows, send, recv):
+        me = slot(g, pitch, rows)
+
+        def one(k, carry):
+            t = peer(k)
+            remote(src.at[slot(t, pitch, rows)], dst.at[me], send, recv, grid=t).start()
+            return carry
+
+        lax.fori_loop(0, PEERS - 1, one, 0)
+        pltpu.make_async_copy(src.at[me], dst.at[me], sem.at[recv]).start()
+
+    def exchange_cross(src, dst, to, send, recv):
+        me = slot(half * PEERS + g, PITCH_C, ROWS_C)
+        band = to * 2 + core
+
+        def copy(t):
+            here = slot(to * PEERS + t, PITCH_C, ROWS_C)
+            return remote(src.at[here], dst.at[me], send, recv, band=band, grid=t)
+
+        @pl.when(to == half)
+        def _():
+            pltpu.make_async_copy(src.at[me], dst.at[me], sem.at[recv]).start()
+
+        @pl.when(to != half)
+        def _():
+            copy(g).start()
+
+        def one(k, carry):
+            copy(peer(k)).start()
+            return carry
+
+        lax.fori_loop(0, PEERS - 1, one, 0)
+
+    def arrived(dst, rows, recv):
+        whole = dst.at[pl.ds(0, rows)]
+        pltpu.make_async_copy(whole, whole, sem.at[recv]).wait()
+
+    pl.semaphore_wait(sem_xy, 15)
+    exchange(f_s1, f_r1, PITCH_1, ROWS_1, F1S, F1R)
+
     @pl.when(core == 0)
     def _():
         mask_copies(lambda c: c.start(), lambda c: c.start())
 
-    def slot(index, pitch, rows):
-        return pl.ds(pl.multiple_of(index * pitch, pitch), rows)
-
-    def exchange_own(src, dst, send, recv):
-        def one(k, carry):
-            t = lax.rem(g + k, PEERS)
-            remote(
-                src.at[slot(t, PITCH_O, ROWS_O)], dst.at[slot(g, PITCH_O, ROWS_O)], send, recv, grid=t
-            ).start()
-            return carry
-
-        lax.fori_loop(1, PEERS, one, 0)
-        me = slot(g, PITCH_O, ROWS_O)
-        pltpu.make_async_copy(src.at[me], dst.at[me], sem.at[recv]).start()
-
-    def exchange_cross(src, dst, send, recv):
-        index = half * PEERS + g
-        me = slot(index, PITCH_C, ROWS_C)
-
-        def one(k, carry):
-            t = lax.rem(index + k, 2 * PEERS)
-            remote(
-                src.at[slot(t, PITCH_C, ROWS_C)], dst.at[me], send, recv,
-                band=(t // PEERS) * 2 + core, grid=t % PEERS,
-            ).start()
-            return carry
-
-        lax.fori_loop(1, 2 * PEERS, one, 0)
-        pltpu.make_async_copy(src.at[me], dst.at[me], sem.at[recv]).start()
-
-    def arrived(dst, rows, recv):
-        whole = dst.at[pl.ds(0, rows)]
-        pltpu.make_async_copy(whole, whole, sem.at[recv]).wait()
-
-    exchange_own(f_so, f_ro, FOS, FOR)
-
+    v0, v1 = core, 1 - core
+    to_core.wait_recv()
+    real, imag = forward_planes(
+        [u[0, p] * v[v0, p] for p in range(2)] + [u[1, p] * v[v1, p] for p in range(2)], ty, wz
+    )
+    for p in range(2):
+        chunks = to_chunks(quarters([real[p], real[2 + p], imag[p], imag[2 + p]]))
+        store_chunks(f_s2, PITCH_2, lambda j: j * 2 + p, chunks)
+
+    first_quad = half * core
+    quads = ((first_quad, 0, core), (1 - first_quad, 1, 1 - core))
+
+    def pack_cross(quad, f, n):
+        near = [chip[n, i, half] for i in (0, half, 1 - half, 1)]
+        d = [a * far[f, i] for a, i in zip(near, (0, 1 - half, half, 1))]
+        pack_quad(f_sc, PITCH_C, quad * (PEERS * PITCH_C), *forward_planes(d, ty, wz))
+
+    to_half.wait_recv()
+    far_to_core = remote(far.at[0], far.at[1], E3S, E3R, band=other_core)
+    far_to_core.start()
+    pack_cross(*quads[0])
+    exchange_cross(f_sc, f_rc, quads[0][0], FCS, FCR)
+    far_to_core.wait_recv()
+    pack_cross(*quads[1])
+    exchange_cross(f_sc, f_rc, quads[1][0], FCS, FCR)
+
+    exchange(f_s2, f_r2, PITCH_2, ROWS_2, F2S, F2R)
     @pl.when(core == 0)
     def _():
         for j in range(3):
@@ -490,49 +568,35 @@
 
     kernel_of = [kernel_table(mask_recv[j], *piece_of(g, j)) for j in range(3)]
 
-    first_quad = half * core
-    quads = ((first_quad, 0, core), (1 - first_quad, 1, 1 - core))
-
-    def pack_cross(quad, f, n):
-        near = [chip[n, i, half] for i in (0, half, 1 - half, 1)]
-        d = [a * far[f, i] for a, i in zip(near, (0, 1 - half, half, 1))]
-        pack_quad(f_sc, PITCH_C, quad * (PEERS * PITCH_C), *forward_planes(d, ty, wz))
-
-    to_half.wait_recv()
-    far_to_core = remote(far.at[0], far.at[1], E3S, E3R, band=other_core)
-    far_to_core.start()
-    pack_cross(*quads[0])
-    far_to_core.wait_recv()
-    pack_cross(*quads[1])
-    exchange_cross(f_sc, f_rc, FCS, FCR)
-
-    arrived(f_ro, PEERS * ROWS_O, FOR)
-    middle_quad(f_ro, b_so, PITCH_O, 6, kernel_of, tx, txi)
-    middle_single(f_ro, b_so, PITCH_O, kernel_of, tx, txi)
-    exchange_own(b_so, b_ro, BOS, BOR)
+    arrived(f_r1, PEERS * ROWS_1, F1R)
+    middle_first(f_r1, b_s1, kernel_of, tx, txi)
+    exchange(b_s1, b_r1, PITCH_1, ROWS_1, B1S, B1R)
+    arrived(f_r2, PEERS * ROWS_2, F2R)
+    middle_second(f_r2, b_s2, kernel_of, tx, txi)
     arrived(f_rc, 2 * PEERS * ROWS_C, FCR)
-    middle_quad(f_rc, b_sc, PITCH_C, PEERS * PITCH_C, kernel_of, tx, txi)
-    exchange_cross(b_sc, b_rc, BCS, BCR)
+    middle_cross(f_rc, b_sc, kernel_of, tx, txi)
+    exchange_cross(b_sc, b_rc, half, BCS, BCR)
+    exchange_cross(b_sc, b_rc, 1 - half, BCS, BCR)
 
     mine = half * 4 + core * 2
     theirs = half * 4 + (1 - core) * 2
-    arrived(b_ro, PEERS * ROWS_O, BOR)
-    q = quarters(from_chunks(load_chunks(b_ro, PITCH_O, lambda j: 12 + j)))
-    lone = inverse_planes([q[0], q[2]], [q[1], q[3]], wzi, tyi)
+    arrived(b_r1, PEERS * ROWS_1, B1R)
+    rest = unpack(b_r1, PITCH_1, lambda j: j * 3 + 2)
     for p in range(2):
-        pot = inverse_planes(*unpack_quad(b_ro, PITCH_O, p * 6), wzi, tyi)
-        u0, u1 = u[0, p], u[1, p]
-        o0, o1 = occ[mine] * u0, occ[mine + 1] * u1
-        act[0, p] = o0 * pot[0] + o1 * pot[1] + occ[theirs + v0] * v[v0, p] * pot[3]
-        act[1, p] = o0 * pot[1] + o1 * pot[2] + occ[theirs + v1] * v[v1, p] * lone[p]
-        pv[v0, p] = o0 * pot[3]
-        pv[v1, p] = o1 * lone[p]
-
+        parts = unpack(b_r1, PITCH_1, lambda j: j * 3 + p)
+        pot = inverse_planes(parts[:3], parts[3:] + rest[2 * p : 2 * p + 2], wzi, tyi)
+        o0, o1 = occ[mine] * u[0, p], occ[mine + 1] * u[1, p]
+        act[0, p] = o0 * pot[0] + o1 * pot[1]
+        act[1, p] = o0 * pot[1] + o1 * pot[2]
+
+    pv[...] = jnp.zeros_like(pv)
     arrived(b_rc, 2 * PEERS * ROWS_C, BCR)
 
+    exchange(b_s2, b_r2, PITCH_2, ROWS_2, B2S, B2R)
     def cross_terms(quad, f, n):
         first = quad * (PEERS * PITCH_C)
-        p00, p01, p10, p11 = inverse_planes(*unpack_quad(b_rc, PITCH_C, first), wzi, tyi)
+        real, imag = (unpack(b_rc, PITCH_C, lambda j: first + j * 2 + ri) for ri in range(2))
+        p00, p01, p10, p11 = inverse_planes(real, imag, wzi, tyi)
         p01, p10 = jnp.where(half == 0, p01, p10), jnp.where(half == 0, p10, p01)
         here = half * 4 + jnp.where(n == 0, core, 1 - core) * 2
         there = (1 - half) * 4 + (core if f == 0 else 1 - core) * 2
@@ -549,8 +613,17 @@
     cross_terms(*quads[0])
     merge.wait_recv()
     pf[0] += merged[...]
-    home = remote(pf.at[0], df, DS, DR, band=other_half)
+    home = Cut(pf.at[0], df, DS, DR, other_half)
     home.start()
+
+    arrived(b_r2, PEERS * ROWS_2, B2R)
+    for p in range(2):
+        a_re, b_re, a_im, b_im = unpack(b_r2, PITCH_2, lambda j: j * 2 + p)
+        pot = inverse_planes([a_re, b_re], [a_im, b_im], wzi, tyi)
+        act[0, p] += occ[theirs + v0] * v[v0, p] * pot[0]
+        act[1, p] += occ[theirs + v1] * v[v1, p] * pot[1]
+        pv[v0, p] += occ[mine] * u[0, p] * pot[0]
+        pv[v1, p] += occ[mine + 1] * u[1, p] * pot[1]
     swap = remote(pv, pvr, E2S, E2R, band=other_core)
     swap.start()
     swap.wait_recv()
@@ -570,9 +643,11 @@
         mask_copies(lambda c: c.wait_send(), None)
 
     for src, rows, send in (
-        (f_so, (PEERS - 1) * ROWS_O, FOS),
+        (f_s1, (PEERS - 1) * ROWS_1, F1S),
+        (f_s2, (PEERS - 1) * ROWS_2, F2S),
         (f_sc, (2 * PEERS - 1) * ROWS_C, FCS),
-        (b_so, (PEERS - 1) * ROWS_O, BOS),
+        (b_s1, (PEERS - 1) * ROWS_1, B1S),
+        (b_s2, (PEERS - 1) * ROWS_2, B2S),
         (b_sc, (2 * PEERS - 1) * ROWS_C, BCS),
     ):
         arrived(src, rows, send)
@@ -587,22 +662,25 @@
     twice = pltpu.VMEM((2, 2, 2, N, N), jnp.float32)
     plane = pltpu.VMEM((2, N, N), jnp.float32)
     planes = pltpu.VMEM((2, 2, N, N), jnp.float32)
-    message = pltpu.VMEM((PEERS * PITCH_O, 128), jnp.float32)
+    messages = [
+        pltpu.VMEM((slots * pitch, 128), jnp.float32)
+        for slots, pitch in ((PEERS, PITCH_1), (PEERS, PITCH_2), (2 * PEERS, PITCH_C))
+        for _ in range(4)
+    ]
     tables = make_tables()
     loaded = [twice, pltpu.VMEM(kept_modes.shape, jnp.int32)]
     loaded += [pltpu.VMEM(t.shape, jnp.bfloat16) for t in tables]
     return pl.pallas_call(
         body,
         out_shape=jax.ShapeDtypeStruct(orbitals.shape, jnp.float32),
-        in_specs=[pl.BlockSpec(memory_space=pltpu.SMEM)] + [pl.BlockSpec(memory_space=pl.ANY)] * 9,
+        in_specs=[pl.BlockSpec(memory_space=pltpu.SMEM)] + [pl.BlockSpec(memory_space=pltpu.HBM)] * 9,
         out_specs=pl.BlockSpec(memory_space=pltpu.VMEM),
         scratch_shapes=loaded
         + [planes, block, plane, plane, twice, planes]
         + [pltpu.VMEM((8, 32, 128), jnp.float32), pltpu.VMEM((3, 32, 128), jnp.float32)]
-        + [message] * 8
+        + messages
         + [
             pltpu.SemaphoreType.DMA((NSEM,)),
-            pltpu.SemaphoreType.REGULAR,
             pltpu.SemaphoreType.REGULAR,
         ],
         compiler_params=pltpu.CompilerParams(

time: 74 us -> 71.9 us (0.972)
  the two profiles are of different devices: /device:TPU:1 before, /device:TPU:32 now
where the time goes in v2:
time: 71.9 us; the launch traced here: 71.8 us
  Pallas kernels  70.1 us (97%)
  local copies, waits for them, and re-layouts  1.67 us (2%)
    pallas_call x1, Pallas kernels, on_device(): pl.pallas_call(body, out_shape=jax.ShapeDtypeStruct(orbitals.shape, jnp.f...  70.1 us
    unnamed x1, local copies, waits for them, and re-layouts  1.67 us

profile of v2, /device:TPU:32, one launch (start us, length us, event | category | flops | bytes accessed | tf_op | source)
XLA Modules:
  0.0 71.8 jit_solution(14429907562971535935)
XLA Ops:
  0.0 70.1 %exchange.1 = f32[2,2,128,128]{3,2,1,0:T(8,128)} custom-call(f32[8]{0:T(128)} %occ.1, f32[2,2,128,128]{3,2,1,0:T(8,128)} %orb_in.1, s32[128,2,128]{2,1,0:T(2,128)} %kept_in.1, bf16[128,384]{1,0:T(8,128)(2,1)} %constant.14.clone.ty_in, bf16[384,256]{1,0:T(8,128)(2,1)} %constant.15.clone.wz_in, bf16[384,256]{1,0:T(8,128)(2,1)} %constant.16.clone.wzi_in, ...), custom_call_target="tpu_custom_call" | custom-call | tf_op jit(solution)/shard_map/exchange/pallas_call | solution.py:673
  70.1 1.7 %copy.12 = f32[2,2,128,128]{3,2,1,0:T(8,128)} copy(f32[2,2,128,128]{3,2,1,0:T(8,128)} %exchange.1) | data formatting | bytes 524288

commit v3 on v2

--- a/solution.py
+++ b/solution.py
@@ -13,31 +13,35 @@
 MESH = pl.DeviceIdType.MESH
 N = 128
 PEERS = 64
-ROWS_1, PITCH_1 = 9, 16
-ROWS_2, PITCH_2 = 6, 8
-ROWS_C, PITCH_C = 6, 8
+PIECE_1, PITCH_1 = 3, 16
+PIECE_2, PITCH_2 = 2, 8
+PIECE_C, PITCH_C = 2, 8
+CHUNKS = 23
+OWN_THREE = 49
+PIECES = 3 * OWN_THREE + 2 * (PEERS - OWN_THREE)
 LAST_KEPT = 57
 CUTS = 8
 
 E1S, E1R, AS, AR, F1S, F1R, F2S, F2R, FCS, FCR, B1S, B1R, B2S, B2R, BCS, BCR = range(16)
 E2S, E2R, E3S, E3R, X1S, X1R, DS, DR, MFS, MFR = range(16, 26)
 MR = 26
-MS = 29
-LS = 37
-NSEM = 46
+MS = 30
+LS = 38
+NSEM = 47
 
 
 def row_order():
     order = list(range(24)) + [31] + list(range(24, 31)) + list(range(32, 48))
-    order += [48, 55] + list(range(49, 55)) + [57, 56]
+    order += [54, 52, 53, 55, 48, 49, 50, 51] + [57, -1, -1, 56] + [-1] * 4
     return order
 
 
 def lane_order():
     out = []
     for q in range(4):
-        out += [16 * q + i for i in range(16)]
-        out += [-16 * q - 16 + i for i in range(16)]
+        for first in (16 * q, 16 * q + 8):
+            out += [first + i for i in range(8)]
+            out += [-first - 1 - i for i in range(8)]
     return out
 
 
@@ -64,12 +68,12 @@
     turn = 2.0 * np.pi / N
     angle_y = turn * ((ky[:, None] * n[None, :]) % N)
     forward_y = np.zeros((128, N))
-    forward_y[: len(ky)] = np.cos(angle_y)
-    forward_y[64 : 64 + len(ky)] = -np.sin(angle_y)
-    weight = np.where(ky == 0, 1.0, 2.0)[:, None]
+    forward_y[:64] = np.where(ky < 0, 0.0, 1.0)[:, None] * np.cos(angle_y)
+    forward_y[64:] = -np.where(ky < 0, 0.0, 1.0)[:, None] * np.sin(angle_y)
+    weight = np.where(ky < 0, 0.0, np.where(ky == 0, 1.0, 2.0))[:, None]
     inverse_y = np.zeros((128, N))
-    inverse_y[: len(ky)] = weight * np.cos(angle_y)
-    inverse_y[64 : 64 + len(ky)] = -weight * np.sin(angle_y)
+    inverse_y[:64] = weight * np.cos(angle_y)
+    inverse_y[64:] = -weight * np.sin(angle_y)
     inverse_y = inverse_y.T
     angle_z = turn * ((n[:, None] * kz[None, :]) % N)
     forward_z = np.concatenate([np.cos(angle_z), np.sin(angle_z)], axis=1)
@@ -142,23 +146,35 @@
     def chunk(g, c):
         return q[g][8 * c : 8 * c + 8]
 
+    def merge(first, second):
+        return jnp.where(inner, first, turn_lanes(second, 16))
+
     sub = sublane_ids()
-    mixed_x = jnp.where(sub == 0, chunk(0, 7), chunk(3, 3))
-    mixed_y = jnp.where(sub == 1, chunk(0, 7), chunk(1, 6))
+    inner = lane_ids(8) % 32 < 16
+    x = merge(chunk(3, 2), jnp.where(sub == 0, chunk(1, 6), chunk(3, 3)))
+    y = merge(chunk(2, 5), jnp.where(sub < 3, chunk(1, 6), chunk(3, 1)))
+    y = jnp.where(sub == 0, chunk(2, 5), y)
+    z = jnp.where(sub < 3, chunk(3, 1), jnp.where(sub == 3, chunk(0, 7), chunk(1, 6)))
     out = [chunk(0, c) for c in range(7)] + [chunk(1, c) for c in range(6)]
-    out += [chunk(2, c) for c in range(6)] + [chunk(3, c) for c in range(3)]
-    return out + [mixed_x, mixed_y]
+    out += [chunk(2, c) for c in range(5)] + [chunk(3, 0)]
+    return out + [x, y, z, chunk(0, 7)]
 
 
 def from_chunks(chunks):
     sub = sublane_ids()
+    inner = lane_ids(8) % 32 < 16
     zero = jnp.zeros((8, 128), jnp.float32)
-    mixed_x, mixed_y = chunks[22], chunks[23]
-    last = jnp.where(sub == 0, mixed_x, jnp.where(sub == 1, mixed_y, zero))
-    q0 = chunks[0:7] + [last]
-    q1 = chunks[7:13] + [jnp.where(sub == 1, zero, mixed_y), zero]
-    q2 = chunks[13:19] + [zero, zero]
-    q3 = chunks[19:22] + [jnp.where(sub == 0, zero, mixed_x)] + [zero] * 4
+    x, y, z, last = chunks[19:]
+    x_second = jnp.where(inner, turn_lanes(x, -16), zero)
+    y_second = jnp.where(inner, turn_lanes(y, -16), zero)
+    x_first = jnp.where(inner, x, zero)
+    y_first = jnp.where(inner | (sub == 0), y, zero)
+    q0 = chunks[0:7] + [jnp.where(sub == 0, last, jnp.where(sub == 3, z, zero))]
+    mixed = jnp.where(sub == 0, x_second, jnp.where(sub < 3, y_second, jnp.where(sub == 3, zero, z)))
+    q1 = chunks[7:13] + [mixed, zero]
+    q2 = chunks[13:18] + [y_first, zero, zero]
+    q3 = [chunks[18], jnp.where(sub < 3, z, y_second), x_first, jnp.where(sub == 0, zero, x_second)]
+    q3 += [zero] * 4
     return [jnp.concatenate(parts, axis=0) for parts in (q0, q1, q2, q3)]
 
 
@@ -189,7 +205,7 @@
 
 
 def load_chunks(buf, pitch, row):
-    return [buf[pl.ds((m % 8) * 8 * pitch + row(m // 8), 8, stride=pitch), :] for m in range(24)]
+    return [buf[pl.ds((m % 8) * 8 * pitch + row(m // 8), 8, stride=pitch), :] for m in range(CHUNKS)]
 
 
 def pack_quad(buf, pitch, first, real, imag):
@@ -280,55 +296,86 @@
             send[pl.ds(j * 2 + plane, 64, stride=PITCH_2), :] = new[64 * plane : 64 * plane + 64]
 
 
-def piece_of(t, j):
-    m = j * 8 + t // 8
-    sub = t % 8
-    q = jnp.where(m < 7, 0, jnp.where(m < 13, 1, jnp.where(m < 19, 2, 3)))
-    c = m - jnp.where(m < 7, 0, jnp.where(m < 13, 7, jnp.where(m < 19, 13, 19)))
-    is_x = m == 22
-    is_y = m == 23
-    q = jnp.where(is_y, 1, q)
-    c = jnp.where(is_x, 3, jnp.where(is_y, 6, c))
-    extra = (is_x & (sub == 0)) | (is_y & (sub == 1))
-    q = jnp.where(extra, 0, q)
-    c = jnp.where(extra, 7, c)
-    pos = c * 8 + sub
+def place_of(g):
+    line = g // 4
+    return 16 * ((g % 4 + 3 - line % 4) % 4) + line
+
+
+def frequency_at(pos):
     ky = jnp.where((pos >= 25) & (pos <= 31), pos - 1, pos)
-    ky = jnp.where((pos >= 50) & (pos <= 55), pos - 1, ky)
-    ky = jnp.where(pos == 24, 31, ky)
-    ky = jnp.where(pos == 49, 55, ky)
-    ky = jnp.where(pos == 56, 57, ky)
-    ky = jnp.where(pos == 57, 56, ky)
-    return ky, q
+    ky = jnp.where((pos >= 52) & (pos <= 55), pos - 4, ky)
+    for at, value in ((24, 31), (48, 54), (49, 52), (50, 53), (51, 55), (56, 57), (59, 56)):
+        ky = jnp.where(pos == at, value, ky)
+    return ky
+
+
+def position_of(ky):
+    pos = jnp.where((ky >= 24) & (ky <= 30), ky + 1, ky)
+    pos = jnp.where((ky >= 48) & (ky <= 51), ky + 4, pos)
+    for at, value in ((24, 31), (48, 54), (49, 52), (50, 53), (51, 55), (56, 57), (59, 56)):
+        pos = jnp.where(ky == value, at, pos)
+    return pos
+
+
+def pick(cases, otherwise):
+    out = otherwise
+    for condition, case in reversed(cases):
+        out = jnp.where(condition, case, out)
+    return out
+
+
+def piece_of(place, j):
+    m = j * 8 + place // 8
+    sub = place % 8
+    in_z = m == 21
+    cases = [
+        (m < 7, 0), (m < 13, 1), (m < 18, 2), (m < 20, 3), (m == 20, 2),
+        (in_z & (sub < 3), 3), (in_z & (sub > 3), 1),
+    ]
+    q = pick(cases, 0)
+    cases = [
+        (m < 7, m), (m < 13, m - 7), (m < 18, m - 13), (m == 18, 0), (m == 19, 2), (m == 20, 5),
+        (in_z & (sub < 3), 1), (in_z & (sub > 3), 6),
+    ]
+    c = pick(cases, 7)
+    merged = (m == 19) | ((m == 20) & (sub > 0))
+    from_1 = ((m == 19) & (sub == 0)) | ((m == 20) & (sub < 3))
+    q_outer = jnp.where(merged, jnp.where(from_1, 1, 3), q)
+    c_outer = jnp.where(merged, jnp.where(from_1, 6, jnp.where(m == 19, 3, 1)), c)
+    inner = (frequency_at(c * 8 + sub), q)
+    return inner, (frequency_at(c_outer * 8 + sub), q_outer), merged
 
 
 def owner_of(ky, q):
-    pos = jnp.where((ky >= 24) & (ky <= 30), ky + 1, ky)
-    pos = jnp.where((ky >= 49) & (ky <= 54), ky + 1, pos)
-    pos = jnp.where(ky == 31, 24, pos)
-    pos = jnp.where(ky == 55, 49, pos)
-    pos = jnp.where(ky == 57, 56, pos)
-    pos = jnp.where(ky == 56, 57, pos)
+    pos = position_of(ky)
     c = pos // 8
     sub = pos % 8
-    full = jnp.where(q == 0, 7, jnp.where(q == 3, 3, 6))
-    base = jnp.where(q == 0, 0, jnp.where(q == 1, 7, jnp.where(q == 2, 13, 19)))
-    m = base + c
-    m = jnp.where((q == 0) & (c == 7), 22 + sub, m)
-    m = jnp.where((q == 1) & (c == 6), 23, m)
-    m = jnp.where((q == 3) & (c == 3), 22, m)
+    cases = [
+        ((q == 0) & (c < 7), c), ((q == 0) & (sub == 0), 22), (q == 0, 21),
+        ((q == 1) & (c < 6), c + 7), ((q == 1) & (sub == 0), 19), ((q == 1) & (sub < 3), 20),
+        (q == 1, 21), ((q == 2) & (c < 5), c + 13), (q == 2, 20),
+        (c == 0, 18), ((c == 1) & (sub < 3), 21), (c == 1, 20),
+    ]
+    m = pick(cases, 19)
+    second = ((q == 1) & (c == 6) & (sub < 3)) | (
+        (q == 3) & (((c == 1) & (sub >= 3)) | (c == 3))
+    )
     exists = (
-        (c < full)
-        | ((q == 0) & (c == 7))
-        | ((q == 1) & (c == 6) & (sub != 1))
-        | ((q == 3) & (c == 3) & (sub != 0))
+        (q == 0)
+        | ((q == 1) & ((c < 6) | ((c == 6) & (sub != 3))))
+        | ((q == 2) & (c < 6))
+        | ((q == 3) & ((c < 3) | ((c == 3) & (sub > 0))))
     ) & (ky <= LAST_KEPT)
     m = jnp.where(exists, m, 0)
-    return exists, (m % 8) * 8 + sub, m // 8
-
-
-def kernel_table(mask, ky, q):
+    place = (m % 8) * 8 + sub
+    line = place % 16
+    return exists, line * 4 + (place // 16 + 1 + line) % 4, jnp.where(second, 3, m // 8)
+
+
+def kernel_table(mask, second, piece):
+    (ky_inner, q_inner), (ky_outer, q_outer), merged = piece
     lane = lane_ids(32)
+    mask = jnp.where((lane % 32 >= 16) & merged, turn_lanes(second, 16), mask)
     rows = []
     for block in range(4):
         part = jnp.where(lane // 32 == block, mask, 0.0)
@@ -337,8 +384,11 @@
     kept = jnp.concatenate(rows, axis=0)
     kx = lax.broadcasted_iota(jnp.int32, (128, 128), 0)
     kx = jnp.where(kx < 64, kx, kx - 128)
-    i = lane_ids(128) % 32
-    kz = jnp.where(i < 16, 16 * q + i, i - 32 - 16 * q)
+    inner = lane_ids(128) % 32 < 16
+    i = lane_ids(128) % 16
+    ky = jnp.where(inner, ky_inner, ky_outer)
+    first = jnp.where(inner, 16 * q_inner, 16 * q_outer + jnp.where(merged, 0, 8))
+    kz = jnp.where(i < 8, first + i, 7 - first - i)
     squared = kx * kx + ky * ky + kz * kz
     safe = jnp.maximum(squared, 1).astype(jnp.float32)
     return jnp.where(squared > 0, (8.0 * math.pi / N**3) / safe, 0.0) * kept
@@ -356,6 +406,7 @@
     other_core = half * 2 + (1 - core)
     other_half = (1 - half) * 2 + core
 
+    mask_recv[...] = jnp.zeros_like(mask_recv)
     u, v = chip.at[0], chip.at[1]
     act, pv = acc.at[0], acc.at[1]
     loads = [
@@ -478,52 +529,109 @@
 
     mask_to_core = remote(mask_recv, mask_recv, MFS, MFR, band=other_core)
 
-    def peer(k):
-        z = (g + jnp.where(k < 16, 2, jnp.where(k < 32, 1, jnp.where(k < 48, 3, 0)))) % 4
-        return ((g // 4 + k + jnp.where(k < 48, 0, 1)) % 16) * 4 + z
-
     def slot(index, pitch, rows):
         return pl.ds(pl.multiple_of(index * pitch, pitch), rows)
 
-    def exchange(src, dst, pitch, rows, send, recv):
-        me = slot(g, pitch, rows)
-
-        def one(k, carry):
-            t = peer(k)
-            remote(src.at[slot(t, pitch, rows)], dst.at[me], send, recv, grid=t).start()
-            return carry
-
-        lax.fori_loop(0, PEERS - 1, one, 0)
-        pltpu.make_async_copy(src.at[me], dst.at[me], sem.at[recv]).start()
-
-    def exchange_cross(src, dst, to, send, recv):
-        me = slot(half * PEERS + g, PITCH_C, ROWS_C)
-        band = to * 2 + core
-
-        def copy(t):
-            here = slot(to * PEERS + t, PITCH_C, ROWS_C)
-            return remote(src.at[here], dst.at[me], send, recv, band=band, grid=t)
+    place = place_of(g)
+    three = place < OWN_THREE
+
+    def sized(count_three, act):
+        @pl.when(count_three)
+        def _():
+            act(3)
+
+        @pl.when(jnp.logical_not(count_three))
+        def _():
+            act(2)
+
+    my_line, my_z = g // 4, g % 4
+    my_first, my_turn = my_line % 4, my_line // 4
+
+    def forward(src, dst, pitch, piece, send, recv, to):
+        there = to * PEERS
+        target_slot = (half * PEERS if dst.shape[0] == 2 * PEERS * pitch else 0) + g
+        source_slot = there if dst.shape[0] == 2 * PEERS * pitch else 0
+
+        def start(pieces, p, t):
+            rows = pieces * piece
+            source, target = src.at[slot(source_slot + p, pitch, rows)], dst.at[slot(target_slot, pitch, rows)]
+            remote(source, target, send, recv, band=to * 2 + core, grid=t).start()
+
+        for step in (2, 1, 3, 0):
+            z = (my_z + step) % 4
+            for r in (1, 2, 3, 0):
+                first = (z + r) % 4
+
+                def one(n, carry):
+                    q = n + my_turn
+                    line = first + 4 * jnp.where(q >= 4, q - 4, q)
+                    p, t = 16 * (3 - r) + line, 4 * line + z
+                    if r > 0:
+                        start(3, p, t)
+                    else:
+                        sized(line == 0, lambda pieces: start(pieces, p, t))
+                    return carry
+
+                if step == 0:
+
+                    @pl.when((first != my_first) | (to != half))
+                    def _():
+                        one(0, 0)
+
+                lax.fori_loop(0 if step > 0 else 1, 4, one, 0)
 
         @pl.when(to == half)
         def _():
-            pltpu.make_async_copy(src.at[me], dst.at[me], sem.at[recv]).start()
-
-        @pl.when(to != half)
-        def _():
-            copy(g).start()
-
-        def one(k, carry):
-            copy(peer(k)).start()
-            return carry
-
-        lax.fori_loop(0, PEERS - 1, one, 0)
+            def local(pieces):
+                rows = pieces * piece
+                source = src.at[slot(source_slot + place, pitch, rows)]
+                pltpu.make_async_copy(source, dst.at[slot(target_slot, pitch, rows)], sem.at[recv]).start()
+
+            sized(three, local)
+
+    def backward(src, dst, pitch, piece, send, recv, to):
+        both = dst.shape[0] == 2 * PEERS * pitch
+        target_slot = (half * PEERS if both else 0) + place
+        source_slot = to * PEERS if both else 0
+
+        def messages(pieces):
+            rows = pieces * piece
+            target = dst.at[slot(target_slot, pitch, rows)]
+
+            def start(t):
+                source = src.at[slot(source_slot + t, pitch, rows)]
+                remote(source, target, send, recv, band=to * 2 + core, grid=t).start()
+
+            for step in (2, 1, 3, 0):
+                z = (my_z + step) % 4
+
+                def one(k, carry):
+                    line = my_line + k
+                    start(4 * jnp.where(line >= 16, line - 16, line) + z)
+                    return carry
+
+                lax.fori_loop(0 if step > 0 else 1, 16, one, 0)
+
+            @pl.when(to != half)
+            def _():
+                start(g)
+
+            @pl.when(to == half)
+            def _():
+                source = src.at[slot(source_slot + g, pitch, rows)]
+                pltpu.make_async_copy(source, target, sem.at[recv]).start()
+
+        sized(three, messages)
+
+    def arrived_own(dst, count, piece, semaphore):
+        sized(three, lambda pieces: arrived(dst, count * pieces * piece, semaphore))
 
     def arrived(dst, rows, recv):
         whole = dst.at[pl.ds(0, rows)]
         pltpu.make_async_copy(whole, whole, sem.at[recv]).wait()
 
     pl.semaphore_wait(sem_xy, 15)
-    exchange(f_s1, f_r1, PITCH_1, ROWS_1, F1S, F1R)
+    forward(f_s1, f_r1, PITCH_1, PIECE_1, F1S, F1R, half)
 
     @pl.when(core == 0)
     def _():
@@ -550,37 +658,42 @@
     far_to_core = remote(far.at[0], far.at[1], E3S, E3R, band=other_core)
     far_to_core.start()
     pack_cross(*quads[0])
-    exchange_cross(f_sc, f_rc, quads[0][0], FCS, FCR)
+    forward(f_sc, f_rc, PITCH_C, PIECE_C, FCS, FCR, quads[0][0])
     far_to_core.wait_recv()
     pack_cross(*quads[1])
-    exchange_cross(f_sc, f_rc, quads[1][0], FCS, FCR)
-
-    exchange(f_s2, f_r2, PITCH_2, ROWS_2, F2S, F2R)
+    forward(f_sc, f_rc, PITCH_C, PIECE_C, FCS, FCR, quads[1][0])
+
+    forward(f_s2, f_r2, PITCH_2, PIECE_2, F2S, F2R, half)
+    two_rows = piece_of(place, 2)[2] & three
     @pl.when(core == 0)
     def _():
-        for j in range(3):
-            pltpu.make_async_copy(mask_recv.at[j], mask_recv.at[j], sem.at[MR + j]).wait()
+        for j, expected in enumerate((True, True, three, two_rows)):
+
+            @pl.when(expected)
+            def _():
+                pltpu.make_async_copy(mask_recv.at[j], mask_recv.at[j], sem.at[MR + j]).wait()
+
         mask_to_core.start()
 
     @pl.when(core == 1)
     def _():
         mask_to_core.wait_recv()
 
-    kernel_of = [kernel_table(mask_recv[j], *piece_of(g, j)) for j in range(3)]
-
-    arrived(f_r1, PEERS * ROWS_1, F1R)
+    kernel_of = [kernel_table(mask_recv[j], mask_recv[3], piece_of(place, j)) for j in range(3)]
+
+    arrived_own(f_r1, PEERS, PIECE_1, F1R)
     middle_first(f_r1, b_s1, kernel_of, tx, txi)
-    exchange(b_s1, b_r1, PITCH_1, ROWS_1, B1S, B1R)
-    arrived(f_r2, PEERS * ROWS_2, F2R)
+    backward(b_s1, b_r1, PITCH_1, PIECE_1, B1S, B1R, half)
+    arrived_own(f_r2, PEERS, PIECE_2, F2R)
     middle_second(f_r2, b_s2, kernel_of, tx, txi)
-    arrived(f_rc, 2 * PEERS * ROWS_C, FCR)
+    arrived_own(f_rc, 2 * PEERS, PIECE_C, FCR)
     middle_cross(f_rc, b_sc, kernel_of, tx, txi)
-    exchange_cross(b_sc, b_rc, half, BCS, BCR)
-    exchange_cross(b_sc, b_rc, 1 - half, BCS, BCR)
+    backward(b_sc, b_rc, PITCH_C, PIECE_C, BCS, BCR, half)
+    backward(b_sc, b_rc, PITCH_C, PIECE_C, BCS, BCR, 1 - half)
 
     mine = half * 4 + core * 2
     theirs = half * 4 + (1 - core) * 2
-    arrived(b_r1, PEERS * ROWS_1, B1R)
+    arrived(b_r1, PIECES * PIECE_1, B1R)
     rest = unpack(b_r1, PITCH_1, lambda j: j * 3 + 2)
     for p in range(2):
         parts = unpack(b_r1, PITCH_1, lambda j: j * 3 + p)
@@ -590,9 +703,9 @@
         act[1, p] = o0 * pot[1] + o1 * pot[2]
 
     pv[...] = jnp.zeros_like(pv)
-    arrived(b_rc, 2 * PEERS * ROWS_C, BCR)
-
-    exchange(b_s2, b_r2, PITCH_2, ROWS_2, B2S, B2R)
+    arrived(b_rc, 2 * PIECES * PIECE_C, BCR)
+
+    backward(b_s2, b_r2, PITCH_2, PIECE_2, B2S, B2R, half)
     def cross_terms(quad, f, n):
         first = quad * (PEERS * PITCH_C)
         real, imag = (unpack(b_rc, PITCH_C, lambda j: first + j * 2 + ri) for ri in range(2))
@@ -616,7 +729,7 @@
     home = Cut(pf.at[0], df, DS, DR, other_half)
     home.start()
 
-    arrived(b_r2, PEERS * ROWS_2, B2R)
+    arrived(b_r2, PIECES * PIECE_2, B2R)
     for p in range(2):
         a_re, b_re, a_im, b_im = unpack(b_r2, PITCH_2, lambda j: j * 2 + p)
         pot = inverse_planes([a_re, b_re], [a_im, b_im], wzi, tyi)
@@ -642,15 +755,15 @@
         mask_to_core.wait_send()
         mask_copies(lambda c: c.wait_send(), None)
 
-    for src, rows, send in (
-        (f_s1, (PEERS - 1) * ROWS_1, F1S),
-        (f_s2, (PEERS - 1) * ROWS_2, F2S),
-        (f_sc, (2 * PEERS - 1) * ROWS_C, FCS),
-        (b_s1, (PEERS - 1) * ROWS_1, B1S),
-        (b_s2, (PEERS - 1) * ROWS_2, B2S),
-        (b_sc, (2 * PEERS - 1) * ROWS_C, BCS),
+    for src, pieces, piece, send in (
+        (f_s1, PIECES, PIECE_1, F1S),
+        (f_s2, PIECES, PIECE_2, F2S),
+        (f_sc, 2 * PIECES, PIECE_C, FCS),
     ):
-        arrived(src, rows, send)
+        sized(three, lambda mine: arrived(src, (pieces - mine) * piece, send))
+    arrived_own(b_s1, PEERS - 1, PIECE_1, B1S)
+    arrived_own(b_s2, PEERS - 1, PIECE_2, B2S)
+    arrived_own(b_sc, 2 * PEERS - 1, PIECE_C, BCS)
     far_to_core.wait_send()
     merge.wait_send()
     swap.wait_send()
@@ -677,7 +790,7 @@
         out_specs=pl.BlockSpec(memory_space=pltpu.VMEM),
         scratch_shapes=loaded
         + [planes, block, plane, plane, twice, planes]
-        + [pltpu.VMEM((8, 32, 128), jnp.float32), pltpu.VMEM((3, 32, 128), jnp.float32)]
+        + [pltpu.VMEM((8, 32, 128), jnp.float32), pltpu.VMEM((4, 32, 128), jnp.float32)]
         + messages
         + [
             pltpu.SemaphoreType.DMA((NSEM,)),

time: 71.9 us -> 70.1 us (0.975)
  Pallas kernels: 70.1 us -> 68.3 us
    pallas_call x1, Pallas kernels: 70.1 us -> 68.3 us  [on_device(): pl.pallas_call(body, out_shape=jax.ShapeDtypeStruct(orbitals.shape, jnp.f...]
where the time goes in v3:
time: 70.1 us; the launch traced here: 70 us
  Pallas kernels  68.3 us (97%)
  local copies, waits for them, and re-layouts  1.67 us (2%)
    pallas_call x1, Pallas kernels, on_device(): pl.pallas_call(body, out_shape=jax.ShapeDtypeStruct(orbitals.shape, jnp.f...  68.3 us
    unnamed x1, local copies, waits for them, and re-layouts  1.67 us

profile of v3, /device:TPU:32, one launch (start us, length us, event | category | flops | bytes accessed | tf_op | source)
XLA Modules:
  0.0 70.0 jit_solution(16291692810610054145)
XLA Ops:
  0.0 68.3 %exchange.1 = f32[2,2,128,128]{3,2,1,0:T(8,128)} custom-call(f32[8]{0:T(128)} %occ.1, f32[2,2,128,128]{3,2,1,0:T(8,128)} %orb_in.1, s32[128,2,128]{2,1,0:T(2,128)} %kept_in.1, bf16[128,384]{1,0:T(8,128)(2,1)} %constant.14.clone.ty_in, bf16[384,256]{1,0:T(8,128)(2,1)} %constant.15.clone.wz_in, bf16[384,256]{1,0:T(8,128)(2,1)} %constant.16.clone.wzi_in, ...), custom_call_target="tpu_custom_call" | custom-call | tf_op jit(solution)/shard_map/exchange/pallas_call | solution.py:786
  68.3 1.7 %copy.12 = f32[2,2,128,128]{3,2,1,0:T(8,128)} copy(f32[2,2,128,128]{3,2,1,0:T(8,128)} %exchange.1) | data formatting | bytes 524288

commit v4 on v3

--- a/solution.py
+++ b/solution.py
@@ -23,11 +23,11 @@
 CUTS = 8
 
 E1S, E1R, AS, AR, F1S, F1R, F2S, F2R, FCS, FCR, B1S, B1R, B2S, B2R, BCS, BCR = range(16)
-E2S, E2R, E3S, E3R, X1S, X1R, DS, DR, MFS, MFR = range(16, 26)
-MR = 26
-MS = 30
-LS = 38
-NSEM = 47
+E2S, E2R, E3S, E3R, X1S, X1R, DS, DR, MFS, MFR, BOR = range(16, 27)
+MR = 27
+MS = 31
+LS = 39
+NSEM = 48
 
 
 def row_order():
@@ -688,8 +688,8 @@
     middle_second(f_r2, b_s2, kernel_of, tx, txi)
     arrived_own(f_rc, 2 * PEERS, PIECE_C, FCR)
     middle_cross(f_rc, b_sc, kernel_of, tx, txi)
+    backward(b_sc, b_rc, PITCH_C, PIECE_C, BCS, BOR, 1 - half)
     backward(b_sc, b_rc, PITCH_C, PIECE_C, BCS, BCR, half)
-    backward(b_sc, b_rc, PITCH_C, PIECE_C, BCS, BCR, 1 - half)
 
     mine = half * 4 + core * 2
     theirs = half * 4 + (1 - core) * 2
@@ -703,9 +703,10 @@
         act[1, p] = o0 * pot[1] + o1 * pot[2]
 
     pv[...] = jnp.zeros_like(pv)
-    arrived(b_rc, 2 * PIECES * PIECE_C, BCR)
-
+    arrived(b_rc, PIECES * PIECE_C, BOR)
     backward(b_s2, b_r2, PITCH_2, PIECE_2, B2S, B2R, half)
+    arrived(b_rc, PIECES * PIECE_C, BCR)
+
     def cross_terms(quad, f, n):
         first = quad * (PEERS * PITCH_C)
         real, imag = (unpack(b_rc, PITCH_C, lambda j: first + j * 2 + ri) for ri in range(2))

time: 70.1 us -> 69.1 us (0.986)
  Pallas kernels: 68.3 us -> 67.3 us
    pallas_call x1, Pallas kernels: 68.3 us -> 67.3 us  [on_device(): pl.pallas_call(body, out_shape=jax.ShapeDtypeStruct(orbitals.shape, jnp.f...]
where the time goes in v4:
time: 69.1 us; the launch traced here: 68.9 us
  Pallas kernels  67.3 us (97%)
  local copies, waits for them, and re-layouts  1.67 us (2%)
    pallas_call x1, Pallas kernels, on_device(): pl.pallas_call(body, out_shape=jax.ShapeDtypeStruct(orbitals.shape, jnp.f...  67.3 us
    unnamed x1, local copies, waits for them, and re-layouts  1.67 us

profile of v4, /device:TPU:32, one launch (start us, length us, event | category | flops | bytes accessed | tf_op | source)
XLA Modules:
  0.0 68.9 jit_solution(10994355453886061578)
XLA Ops:
  0.0 67.3 %exchange.1 = f32[2,2,128,128]{3,2,1,0:T(8,128)} custom-call(f32[8]{0:T(128)} %occ.1, f32[2,2,128,128]{3,2,1,0:T(8,128)} %orb_in.1, s32[128,2,128]{2,1,0:T(2,128)} %kept_in.1, bf16[128,384]{1,0:T(8,128)(2,1)} %constant.14.clone.ty_in, bf16[384,256]{1,0:T(8,128)(2,1)} %constant.15.clone.wz_in, bf16[384,256]{1,0:T(8,128)(2,1)} %constant.16.clone.wzi_in, ...), custom_call_target="tpu_custom_call" | custom-call | tf_op jit(solution)/shard_map/exchange/pallas_call | solution.py:787
  67.3 1.7 %copy.12 = f32[2,2,128,128]{3,2,1,0:T(8,128)} copy(f32[2,2,128,128]{3,2,1,0:T(8,128)} %exchange.1) | data formatting | bytes 524288

commit v5 on v4

--- a/solution.py
+++ b/solution.py
@@ -20,7 +20,7 @@
 OWN_THREE = 49
 PIECES = 3 * OWN_THREE + 2 * (PEERS - OWN_THREE)
 LAST_KEPT = 57
-CUTS = 8
+CUTS = 2
 
 E1S, E1R, AS, AR, F1S, F1R, F2S, F2R, FCS, FCR, B1S, B1R, B2S, B2R, BCS, BCR = range(16)
 E2S, E2R, E3S, E3R, X1S, X1R, DS, DR, MFS, MFR, BOR = range(16, 27)
@@ -549,16 +549,18 @@
 
     def forward(src, dst, pitch, piece, send, recv, to):
         there = to * PEERS
-        target_slot = (half * PEERS if dst.shape[0] == 2 * PEERS * pitch else 0) + g
-        source_slot = there if dst.shape[0] == 2 * PEERS * pitch else 0
+        both = dst.shape[0] > (PEERS + 1) * pitch
+        target_slot = (half * PEERS if both else 0) + g
+        source_slot = there if both else 0
 
         def start(pieces, p, t):
             rows = pieces * piece
             source, target = src.at[slot(source_slot + p, pitch, rows)], dst.at[slot(target_slot, pitch, rows)]
             remote(source, target, send, recv, band=to * 2 + core, grid=t).start()
 
+        start_z = my_z + jnp.where(to == half, 0, 2)
         for step in (2, 1, 3, 0):
-            z = (my_z + step) % 4
+            z = (start_z + step) % 4
             for r in (1, 2, 3, 0):
                 first = (z + r) % 4
 
@@ -590,7 +592,7 @@
             sized(three, local)
 
     def backward(src, dst, pitch, piece, send, recv, to):
-        both = dst.shape[0] == 2 * PEERS * pitch
+        both = dst.shape[0] > (PEERS + 1) * pitch
         target_slot = (half * PEERS if both else 0) + place
         source_slot = to * PEERS if both else 0
 
@@ -602,8 +604,9 @@
                 source = src.at[slot(source_slot + t, pitch, rows)]
                 remote(source, target, send, recv, band=to * 2 + core, grid=t).start()
 
+            start_z = my_z + jnp.where(to == half, 0, 2)
             for step in (2, 1, 3, 0):
-                z = (my_z + step) % 4
+                z = (start_z + step) % 4
 
                 def one(k, carry):
                     line = my_line + k
@@ -614,7 +617,7 @@
 
             @pl.when(to != half)
             def _():
-                start(g)
+                start(4 * my_line + start_z % 4)
 
             @pl.when(to == half)
             def _():
@@ -777,7 +780,7 @@
     plane = pltpu.VMEM((2, N, N), jnp.float32)
     planes = pltpu.VMEM((2, 2, N, N), jnp.float32)
     messages = [
-        pltpu.VMEM((slots * pitch, 128), jnp.float32)
+        pltpu.VMEM(((slots + 1) * pitch, 128), jnp.float32)
         for slots, pitch in ((PEERS, PITCH_1), (PEERS, PITCH_2), (2 * PEERS, PITCH_C))
         for _ in range(4)
     ]

time: 69.1 us -> 69 us (level)
  no operation moved by 1% of the time
where the time goes in v5:
time: 69 us; the launch traced here: 68.9 us
  Pallas kernels  67.2 us (97%)
  local copies, waits for them, and re-layouts  1.67 us (2%)
    pallas_call x1, Pallas kernels, on_device(): pl.pallas_call(body, out_shape=jax.ShapeDtypeStruct(orbitals.shape, jnp.f...  67.2 us
    unnamed x1, local copies, waits for them, and re-layouts  1.67 us

profile of v5, /device:TPU:32, one launch (start us, length us, event | category | flops | bytes accessed | tf_op | source)
XLA Modules:
  0.0 68.9 jit_solution(4523634115031644506)
XLA Ops:
  0.0 67.2 %exchange.1 = f32[2,2,128,128]{3,2,1,0:T(8,128)} custom-call(f32[8]{0:T(128)} %occ.1, f32[2,2,128,128]{3,2,1,0:T(8,128)} %orb_in.1, s32[128,2,128]{2,1,0:T(2,128)} %kept_in.1, bf16[128,384]{1,0:T(8,128)(2,1)} %constant.14.clone.ty_in, bf16[384,256]{1,0:T(8,128)(2,1)} %constant.15.clone.wz_in, bf16[384,256]{1,0:T(8,128)(2,1)} %constant.16.clone.wzi_in, ...), custom_call_target="tpu_custom_call" | custom-call | tf_op jit(solution)/shard_map/exchange/pallas_call | solution.py:790
  67.2 1.7 %copy.12 = f32[2,2,128,128]{3,2,1,0:T(8,128)} copy(f32[2,2,128,128]{3,2,1,0:T(8,128)} %exchange.1) | data formatting | bytes 524288

commit v6 on v5

--- a/solution.py
+++ b/solution.py
@@ -372,8 +372,7 @@
     return exists, line * 4 + (place // 16 + 1 + line) % 4, jnp.where(second, 3, m // 8)
 
 
-def kernel_table(mask, second, piece):
-    (ky_inner, q_inner), (ky_outer, q_outer), merged = piece
+def kernel_table(coulomb, mask, second, merged):
     lane = lane_ids(32)
     mask = jnp.where((lane % 32 >= 16) & merged, turn_lanes(second, 16), mask)
     rows = []
@@ -381,7 +380,11 @@
         part = jnp.where(lane // 32 == block, mask, 0.0)
         part = part + turn_lanes(part, 64)
         rows.append(part + turn_lanes(part, 32))
-    kept = jnp.concatenate(rows, axis=0)
+    return coulomb * jnp.concatenate(rows, axis=0)
+
+
+def coulomb_table(piece):
+    (ky_inner, q_inner), (ky_outer, q_outer), merged = piece
     kx = lax.broadcasted_iota(jnp.int32, (128, 128), 0)
     kx = jnp.where(kx < 64, kx, kx - 128)
     inner = lane_ids(128) % 32 < 16
@@ -391,12 +394,12 @@
     kz = jnp.where(i < 8, first + i, 7 - first - i)
     squared = kx * kx + ky * ky + kz * kz
     safe = jnp.maximum(squared, 1).astype(jnp.float32)
-    return jnp.where(squared > 0, (8.0 * math.pi / N**3) / safe, 0.0) * kept
+    return jnp.where(squared > 0, (8.0 * math.pi / N**3) / safe, 0.0)
 
 
 def body(
     occ, orb_in, kept_in, ty_in, wz_in, wzi_in, tyi_in, tx_in, txi_in, lanes_in, out,
-    chip, kept, ty, wz, wzi, tyi, tx, txi, lanes, far, pvr, df, merged, acc, pf, mask_send, mask_recv,
+    chip, kept, ty, wz, wzi, tyi, tx, txi, lanes, far, pvr, df, merged, acc, pf, mask_send, mask_recv, coulomb,
     f_s1, f_r1, b_s1, b_r1, f_s2, f_r2, b_s2, b_r2, f_sc, f_rc, b_sc, b_rc, sem, sem_xy,
 ):
     b = lax.axis_index("band")
@@ -657,6 +660,9 @@
         d = [a * far[f, i] for a, i in zip(near, (0, 1 - half, half, 1))]
         pack_quad(f_sc, PITCH_C, quad * (PEERS * PITCH_C), *forward_planes(d, ty, wz))
 
+    pieces = [piece_of(place, j) for j in range(3)]
+    for j in range(3):
+        coulomb[j] = coulomb_table(pieces[j])
     to_half.wait_recv()
     far_to_core = remote(far.at[0], far.at[1], E3S, E3R, band=other_core)
     far_to_core.start()
@@ -682,7 +688,9 @@
     def _():
         mask_to_core.wait_recv()
 
-    kernel_of = [kernel_table(mask_recv[j], mask_recv[3], piece_of(place, j)) for j in range(3)]
+    kernel_of = [
+        kernel_table(coulomb[j], mask_recv[j], mask_recv[3], pieces[j][2]) for j in range(3)
+    ]
 
     arrived_own(f_r1, PEERS, PIECE_1, F1R)
     middle_first(f_r1, b_s1, kernel_of, tx, txi)
@@ -795,6 +803,7 @@
         scratch_shapes=loaded
         + [planes, block, plane, plane, twice, planes]
         + [pltpu.VMEM((8, 32, 128), jnp.float32), pltpu.VMEM((4, 32, 128), jnp.float32)]
+        + [pltpu.VMEM((3, N, 128), jnp.float32)]
         + messages
         + [
             pltpu.SemaphoreType.DMA((NSEM,)),

time: 69 us -> 69 us (level)
  no operation moved by 1% of the time
where the time goes in v6:
time: 69 us; the launch traced here: 68.9 us
  Pallas kernels  67.2 us (97%)
  local copies, waits for them, and re-layouts  1.67 us (2%)
    pallas_call x1, Pallas kernels, on_device(): pl.pallas_call(body, out_shape=jax.ShapeDtypeStruct(orbitals.shape, jnp.f...  67.2 us
    unnamed x1, local copies, waits for them, and re-layouts  1.67 us

profile of v6, /device:TPU:32, one launch (start us, length us, event | category | flops | bytes accessed | tf_op | source)
XLA Modules:
  0.0 68.9 jit_solution(351261865254633665)
XLA Ops:
  0.0 67.2 %exchange.1 = f32[2,2,128,128]{3,2,1,0:T(8,128)} custom-call(f32[8]{0:T(128)} %occ.1, f32[2,2,128,128]{3,2,1,0:T(8,128)} %orb_in.1, s32[128,2,128]{2,1,0:T(2,128)} %kept_in.1, bf16[128,384]{1,0:T(8,128)(2,1)} %constant.14.clone.ty_in, bf16[384,256]{1,0:T(8,128)(2,1)} %constant.15.clone.wz_in, bf16[384,256]{1,0:T(8,128)(2,1)} %constant.16.clone.wzi_in, ...), custom_call_target="tpu_custom_call" | custom-call | tf_op jit(solution)/shard_map/exchange/pallas_call | solution.py:798
  67.2 1.7 %copy.12 = f32[2,2,128,128]{3,2,1,0:T(8,128)} copy(f32[2,2,128,128]{3,2,1,0:T(8,128)} %exchange.1) | data formatting | bytes 524288

commit v7 on v6

--- a/solution.py
+++ b/solution.py
@@ -718,7 +718,7 @@
     backward(b_s2, b_r2, PITCH_2, PIECE_2, B2S, B2R, half)
     arrived(b_rc, PIECES * PIECE_C, BCR)
 
-    def cross_terms(quad, f, n):
+    def cross_terms(quad, f, n, send):
         first = quad * (PEERS * PITCH_C)
         real, imag = (unpack(b_rc, PITCH_C, lambda j: first + j * 2 + ri) for ri in range(2))
         p00, p01, p10, p11 = inverse_planes(real, imag, wzi, tyi)
@@ -729,17 +729,20 @@
         f0, f1 = occ[there] * far[f, 0], occ[there + 1] * far[f, 1]
         pf[f, 0] = n0 * p00 + n1 * p10
         pf[f, 1] = n0 * p01 + n1 * p11
+        send()
         acc[n, 0, half] += f0 * p00 + f1 * p01
         acc[n, 1, half] += f0 * p10 + f1 * p11
 
-    cross_terms(*quads[1])
     merge = remote(pf.at[1], merged, X1S, X1R, band=other_core)
-    merge.start()
-    cross_terms(*quads[0])
-    merge.wait_recv()
-    pf[0] += merged[...]
     home = Cut(pf.at[0], df, DS, DR, other_half)
-    home.start()
+
+    def send_home():
+        merge.wait_recv()
+        pf[0] += merged[...]
+        home.start()
+
+    cross_terms(*quads[1], merge.start)
+    cross_terms(*quads[0], send_home)
 
     arrived(b_r2, PIECES * PIECE_2, B2R)
     for p in range(2):

time: 69 us -> 69 us (level)
  no operation moved by 1% of the time
where the time goes in v7:
time: 69 us; the launch traced here: 68.9 us
  Pallas kernels  67.2 us (97%)
  local copies, waits for them, and re-layouts  1.67 us (2%)
    pallas_call x1, Pallas kernels, on_device(): pl.pallas_call(body, out_shape=jax.ShapeDtypeStruct(orbitals.shape, jnp.f...  67.2 us
    unnamed x1, local copies, waits for them, and re-layouts  1.67 us

profile of v7, /device:TPU:32, one launch (start us, length us, event | category | flops | bytes accessed | tf_op | source)
XLA Modules:
  0.0 68.9 jit_solution(2958084172160334748)
XLA Ops:
  0.0 67.2 %exchange.1 = f32[2,2,128,128]{3,2,1,0:T(8,128)} custom-call(f32[8]{0:T(128)} %occ.1, f32[2,2,128,128]{3,2,1,0:T(8,128)} %orb_in.1, s32[128,2,128]{2,1,0:T(2,128)} %kept_in.1, bf16[128,384]{1,0:T(8,128)(2,1)} %constant.14.clone.ty_in, bf16[384,256]{1,0:T(8,128)(2,1)} %constant.15.clone.wz_in, bf16[384,256]{1,0:T(8,128)(2,1)} %constant.16.clone.wzi_in, ...), custom_call_target="tpu_custom_call" | custom-call | tf_op jit(solution)/shard_map/exchange/pallas_call | solution.py:801
  67.2 1.7 %copy.12 = f32[2,2,128,128]{3,2,1,0:T(8,128)} copy(f32[2,2,128,128]{3,2,1,0:T(8,128)} %exchange.1) | data formatting | bytes 524288
